TPU v7x, 32 devices: a whole 2x2x4 slice. The times are simulated.
32 devices in a mesh: fsdp: 4 (over z), ctx: 4 (over x, core), tp: 2 (over y).
Axes of the slice: x: 2, y: 2, z: 4, core: 2. Of those that a mesh axis runs over, the one named last changes fastest.
Arguments:
- tokens: bfloat16 [8192, 1024], P(('fsdp', 'ctx', 'tp')), may hold values from -6 to 6
- cotangent: bfloat16 [8192, 1024], P(('fsdp', 'ctx', 'tp')), may hold values from -6 to 6
- lengths: int32 [4, 12], P('fsdp'), may hold values from 1 to 455, as said below
- dealing: int32 [4, 12], P('fsdp'), may hold values from 0 to 11, as said below
- norm_in: bfloat16 [1024], P('fsdp'), may hold values from 0.5 to 1.5
- w_query: bfloat16 [1024, 512], P('fsdp', 'tp'), may hold values from -0.1875 to 0.1875
- w_keyval: bfloat16 [1024, 2, 128], P('fsdp', 'tp'), may hold values from -0.1875 to 0.1875
- w_attn_out: bfloat16 [512, 1024], P('tp', 'fsdp'), may hold values from -1 to 1
- w_zx: bfloat16 [1024, 2, 1536], P('fsdp', None, 'tp'), may hold values from -0.1875 to 0.1875
- w_bc: bfloat16 [1024, 256], P('fsdp'), may hold values from -0.1875 to 0.1875
- w_step: bfloat16 [1024, 24], P('fsdp', 'tp'), may hold values from -0.1875 to 0.1875
- head_params: float32 [3, 24], P(None, 'tp'), may hold values from -7 to 2.8, as said below
- taps_x: bfloat16 [5, 24, 64], P(None, 'tp', 'fsdp'), may hold values from -0.5 to 0.5
- taps_bc: bfloat16 [5, 256], P(None, 'fsdp'), may hold values from -0.5 to 0.5
- gain_mamba: bfloat16 [24, 64], P('tp', 'fsdp'), may hold values from 0.5 to 1.5
- w_mamba_out: bfloat16 [1536, 1024], P('tp', 'fsdp'), may hold values from -0.15625 to 0.15625
- norm_mid: bfloat16 [1024], P('fsdp'), may hold values from 0.5 to 1.5
- w_gate_up: bfloat16 [1024, 2, 2048], P('fsdp', None, 'tp'), may hold values from -0.1875 to 0.1875
- w_down: bfloat16 [2048, 1024], P('tp', 'fsdp'), may hold values from -0.125 to 0.125
Outputs:
- mixed: bfloat16 [8192, 1024], P(('fsdp', 'ctx', 'tp'))
- grad_tokens: bfloat16 [8192, 1024], P(('fsdp', 'ctx', 'tp'))
- grad_norm_in: float32 [1024], P('fsdp')
- grad_query: float32 [1024, 512], P('fsdp', 'tp')
- grad_keyval: float32 [1024, 2, 128], P('fsdp', 'tp')
- grad_attn_out: float32 [512, 1024], P('tp', 'fsdp')
- grad_zx: float32 [1024, 2, 1536], P('fsdp', None, 'tp')
- grad_bc: float32 [1024, 256], P('fsdp')
- grad_step: float32 [1024, 24], P('fsdp', 'tp')
- grad_heads: float32 [3, 24], P(None, 'tp')
- grad_taps_x: float32 [5, 24, 64], P(None, 'tp', 'fsdp')
- grad_taps_bc: float32 [5, 256], P(None, 'fsdp')
- grad_gain: float32 [24, 64], P('tp', 'fsdp')
- grad_mamba_out: float32 [1536, 1024], P('tp', 'fsdp')
- grad_norm_mid: float32 [1024], P('fsdp')
- grad_gate_up: float32 [1024, 2, 2048], P('fsdp', None, 'tp')
- grad_down: float32 [2048, 1024], P('tp', 'fsdp')
Inputs may be any that keep to these rules, and one draw needn't show every extreme that they name: Each group's lengths sum to 2048; the largest is exactly 455 in every draw. `dealing`: each row is a permutation of the group's sequences; laid end to end in the dealt order, each run of 3 sequences holds exactly 512 tokens. `head_params`: row 0 holds step biases, row 1 logarithms of decay rates, row 2 skip factors.
All inputs are finite; a program needn't handle non-finite values.
Results may differ from a plain program's by a relative error of at most 0.02.
Values may be sent and summed in bfloat16 or wider, within the bound.
No kernel may reach another device: no remote copies, remote signals or barrier semaphores. Data moves between devices by JAX's collectives and lax.ppermute only.
A program may use at most 192 MiB of HBM per device.

v0:
```python
import jax
import jax.numpy as jnp
from jax import lax
from jax.sharding import PartitionSpec as P

HD = 64
BLK = 128


EPSILON = 1e-05
ROPE_BASE = 100000000000.0
PRECISE = lax.Precision.HIGHEST


def round_value(value):
    return lax.optimization_barrier(value.astype(jnp.bfloat16)).astype(jnp.float32)


def round_keep(value):
    return (round_value(value), None)


def round_pass(kept, grad):
    return (grad,)


def plain_value(value):
    return value


def plain_keep(value):
    return (value, None)


def plain_round(kept, grad):
    return (round_value(grad),)


def low(value):
    rounder = jax.custom_vjp(round_value)
    rounder.defvjp(round_keep, round_pass)
    return rounder(value)


def low_back(value):
    keeper = jax.custom_vjp(plain_value)
    keeper.defvjp(plain_keep, plain_round)
    return keeper(value)


def product(left, right):
    return jnp.dot(left, right, precision=PRECISE)


def dealt_rows(lengths, dealing, first_row, row_count):
    seq_count = lengths.shape[0]
    numbers = jnp.arange(seq_count, dtype=jnp.int32)
    given_start = jnp.cumsum(lengths, dtype=jnp.int32) - lengths
    chosen = (dealing[:, None] == numbers[None, :]).astype(jnp.int32)
    dealt_len = jnp.sum(chosen * lengths[None, :], axis=1, dtype=jnp.int32)
    dealt_from = jnp.sum(chosen * given_start[None, :], axis=1, dtype=jnp.int32)
    dealt_start = jnp.cumsum(dealt_len, dtype=jnp.int32) - dealt_len
    spots = first_row + jnp.arange(row_count, dtype=jnp.int32)
    inside = (
        (spots[:, None] >= dealt_start[None, :])
        & (spots[:, None] < (dealt_start + dealt_len)[None, :])
    ).astype(jnp.int32)
    segment = jnp.sum(inside * numbers[None, :], axis=1, dtype=jnp.int32)
    begins = jnp.sum(inside * dealt_start[None, :], axis=1, dtype=jnp.int32)
    anchor = jnp.sum(inside * dealt_from[None, :], axis=1, dtype=jnp.int32)
    position = spots - begins
    return (anchor + position, segment, position)


def rotary(vectors, position):
    half_width = vectors.shape[-1] // 2
    freqs = ROPE_BASE ** (-jnp.arange(half_width, dtype=jnp.float32) / half_width)
    angles = position.astype(jnp.float32)[:, None] * freqs[None, :]
    cosine = jnp.cos(angles)[:, None, :]
    sine_part = jnp.sin(angles)[:, None, :]
    front = vectors[..., :half_width]
    behind = vectors[..., half_width:]
    return jnp.concatenate(
        [front * cosine - behind * sine_part, behind * cosine + front * sine_part], axis=-1
    )


def attend_block(query_part, key_rows, value_rows, query_seg, query_spot, segment, spots):
    head_width = query_part.shape[-1]
    scores = jnp.einsum("igsd,jgd->gsij", query_part, key_rows, precision=PRECISE) * head_width ** (
        -0.5
    )
    scores = low_back(scores)
    allowed = (query_seg[:, None] == segment[None, :]) & (query_spot[:, None] >= spots[None, :])
    scores = jnp.where(allowed[None, None], scores, -1e30)
    peak = jnp.max(scores, axis=-1, keepdims=True)
    weights = jnp.exp(scores - peak)
    probs = low(weights / jnp.sum(weights, axis=-1, keepdims=True))
    return jnp.einsum("gsij,jgd->igsd", probs, value_rows, precision=PRECISE)


def attend(queries, key_rows, value_rows, segment):
    row_total, head_count, head_width = queries.shape
    kv_count = key_rows.shape[1]
    grouped = queries.reshape(row_total, kv_count, head_count // kv_count, head_width)
    spots = jnp.arange(row_total, dtype=jnp.int32)
    block_rows = row_total // 2
    outputs = []
    for block_index in range(2):
        lower = block_index * block_rows
        outputs.append(
            jax.checkpoint(attend_block)(
                grouped[lower : lower + block_rows],
                key_rows,
                value_rows,
                segment[lower : lower + block_rows],
                spots[lower : lower + block_rows],
                segment,
                spots,
            )
        )
    return jnp.concatenate(outputs, axis=0).reshape(row_total, head_count, head_width)


def attention_core(query_raw, keyval_raw, segment, position):
    row_total = query_raw.shape[0]
    queries = low(rotary(query_raw.reshape(row_total, -1, HD), position))
    pairs = keyval_raw.reshape(row_total, -1, 2 * HD)
    key_rows = low(rotary(pairs[..., :HD], position))
    value_rows = low(pairs[..., HD:])
    return attend(queries, key_rows, value_rows, segment).reshape(row_total, -1)


def convolve(signal, taps, position):
    row_total = signal.shape[0]
    width_k = taps.shape[0] - 1
    result = taps[width_k][None, :] + taps[width_k - 1][None, :] * signal
    for lag_index in range(1, width_k):
        moved = jnp.concatenate(
            [
                jnp.zeros((lag_index, signal.shape[1]), signal.dtype),
                signal[: row_total - lag_index],
            ],
            axis=0,
        )
        usable = (position >= lag_index).astype(signal.dtype)[:, None]
        result = result + taps[width_k - 1 - lag_index][None, :] * moved * usable
    return result


def state_space(inputs, b_rows, c_rows, steps, rates, segment):
    row_total, head_count, head_width = inputs.shape
    state_width = b_rows.shape[1]
    block_count = row_total // BLK

    def split_blocks(array):
        return array.reshape((block_count, BLK) + array.shape[1:])

    def advance(carry, pieces):
        states, last_seg = carry
        x_part, b_part, c_part, step_part, seg_part = pieces
        decays = jnp.cumsum(step_part * rates[None, :], axis=0)
        spots = jnp.arange(BLK)
        allowed = (seg_part[:, None] == seg_part[None, :]) & (spots[:, None] >= spots[None, :])
        spread = jnp.where(allowed[:, :, None], decays[:, None, :] - decays[None, :, :], 0.0)
        mixing = jnp.where(allowed[:, :, None], jnp.exp(spread), 0.0)
        inner = product(c_part, b_part.T)
        coupling = mixing * inner[:, :, None] * step_part[None, :, :]
        local_out = jnp.einsum("ijh,jhp->ihp", coupling, x_part, precision=PRECISE)
        carried = (seg_part == last_seg).astype(jnp.float32)[:, None] * jnp.exp(decays)
        recall = jnp.einsum("in,hpn->ihp", c_part, states, precision=PRECISE) * carried[:, :, None]
        tail_seg = seg_part[BLK - 1]
        keeps = (
            (seg_part == tail_seg).astype(jnp.float32)[:, None]
            * jnp.exp(decays[BLK - 1][None, :] - decays)
            * step_part
        )
        fresh = jnp.einsum("jhp,jn->hpn", keeps[:, :, None] * x_part, b_part, precision=PRECISE)
        linger = (tail_seg == last_seg).astype(jnp.float32) * jnp.exp(decays[BLK - 1])
        return ((states * linger[:, None, None] + fresh, tail_seg), local_out + recall)

    start = (jnp.zeros((head_count, head_width, state_width), jnp.float32), jnp.int32(-1))
    pieces = (
        split_blocks(inputs),
        split_blocks(b_rows),
        split_blocks(c_rows),
        split_blocks(steps),
        split_blocks(segment),
    )
    final_carry, outputs = lax.scan(jax.checkpoint(advance), start, pieces)
    return outputs.reshape(row_total, head_count, head_width)


def mamba_gated(gate_in, x_in, bc_in, step_in, taps_x, taps_bc, head_params, segment, position):
    row_total = x_in.shape[0]
    head_count = head_params.shape[1]
    conv_x = low(jax.nn.silu(convolve(x_in, taps_x.reshape(taps_x.shape[0], -1), position)))
    conv_bc = low(jax.nn.silu(convolve(bc_in, taps_bc, position)))
    state_width = conv_bc.shape[1] // 2
    steps = jax.nn.softplus(step_in + head_params[0][None, :])
    rates = -jnp.exp(head_params[1])
    heads_in = conv_x.reshape(row_total, head_count, -1)
    mixed = state_space(
        heads_in, conv_bc[:, :state_width], conv_bc[:, state_width:], steps, rates, segment
    )
    mixed = mixed + head_params[2][None, :, None] * heads_in
    return mixed.reshape(row_total, -1) * jax.nn.silu(gate_in)


def norm_back(grad_out, unit_rows, inverse, gain):
    scaled = grad_out * gain[None, :]
    return inverse * (scaled - unit_rows * jnp.mean(scaled * unit_rows, axis=1, keepdims=True))


def per_device(
    tokens,
    cotangent,
    lengths,
    dealing,
    norm_in,
    w_query,
    w_keyval,
    w_attn_out,
    w_zx,
    w_bc,
    w_step,
    head_params,
    taps_x,
    taps_bc,
    gain_mamba,
    w_mamba_out,
    norm_mid,
    w_gate_up,
    w_down,
):
    tok_rows = tokens.shape[0]
    tp_size = lax.axis_size("tp")
    fsdp_size = lax.axis_size("fsdp")
    rank_rows = tok_rows * tp_size
    tp_index = lax.axis_index("tp")
    fsdp_index = lax.axis_index("fsdp")
    own_start = tp_index * tok_rows
    gathered_tok, gathered_cot = (
        lax.all_gather(tokens, ("ctx", "tp"), axis=0, tiled=True),
        lax.all_gather(cotangent, ("ctx", "tp"), axis=0, tiled=True),
    )
    (
        norm_in,
        w_query,
        w_keyval,
        w_attn_out,
        w_zx,
        w_bc,
        w_step,
        taps_x,
        taps_bc,
        gain_mamba,
        w_mamba_out,
        norm_mid,
        w_gate_up,
        w_down,
    ) = (
        lax.all_gather(norm_in, "fsdp", axis=0, tiled=True),
        lax.all_gather(w_query, "fsdp", axis=0, tiled=True),
        lax.all_gather(w_keyval, "fsdp", axis=0, tiled=True),
        lax.all_gather(w_attn_out, "fsdp", axis=1, tiled=True),
        lax.all_gather(w_zx, "fsdp", axis=0, tiled=True),
        lax.all_gather(w_bc, "fsdp", axis=0, tiled=True),
        lax.all_gather(w_step, "fsdp", axis=0, tiled=True),
        lax.all_gather(taps_x, "fsdp", axis=2, tiled=True),
        lax.all_gather(taps_bc, "fsdp", axis=1, tiled=True),
        lax.all_gather(gain_mamba, "fsdp", axis=1, tiled=True),
        lax.all_gather(w_mamba_out, "fsdp", axis=1, tiled=True),
        lax.all_gather(norm_mid, "fsdp", axis=0, tiled=True),
        lax.all_gather(w_gate_up, "fsdp", axis=0, tiled=True),
        lax.all_gather(w_down, "fsdp", axis=1, tiled=True),
    )
    sources, segment, position = dealt_rows(
        lengths[0], dealing[0], lax.axis_index("ctx") * rank_rows, rank_rows
    )
    x_rows = jnp.take(gathered_tok, sources, axis=0).astype(jnp.float32)
    cot_rows = jnp.take(gathered_cot, sources, axis=0)
    model_width = x_rows.shape[1]
    inverse_in = lax.rsqrt(jnp.mean(x_rows * x_rows, axis=1, keepdims=True) + EPSILON)
    unit_in = x_rows * inverse_in
    normed_in = (unit_in * norm_in[None, :]).astype(jnp.bfloat16)
    query_raw = jnp.dot(normed_in, w_query, preferred_element_type=jnp.float32)
    keyval_raw = jnp.dot(
        normed_in, w_keyval.reshape(model_width, -1), preferred_element_type=jnp.float32
    )

    def attention_local(query_in, keyval_in):
        return attention_core(query_in, keyval_in, segment, position)

    attn_out, attn_pull = jax.vjp(attention_local, query_raw, keyval_raw)
    attn_rows = attn_out.astype(jnp.bfloat16)
    zx_raw = jnp.dot(
        normed_in, w_zx.reshape(model_width, -1), preferred_element_type=jnp.float32
    ).reshape(rank_rows, 2, -1)
    bc_raw = jnp.dot(normed_in, w_bc, preferred_element_type=jnp.float32)
    step_raw = jnp.dot(normed_in, w_step, preferred_element_type=jnp.float32)

    def mamba_local(gate_in, x_in, bc_in, step_in, taps_one, taps_two, heads_one):
        return mamba_gated(
            gate_in, x_in, bc_in, step_in, taps_one, taps_two, heads_one, segment, position
        )

    gated_rows, mamba_pull = jax.vjp(
        mamba_local,
        zx_raw[:, 0],
        zx_raw[:, 1],
        bc_raw,
        step_raw,
        taps_x.astype(jnp.float32),
        taps_bc.astype(jnp.float32),
        head_params,
    )
    channel_total = gated_rows.shape[1] * tp_size
    gain_flat = gain_mamba.astype(jnp.float32).reshape(1, -1)
    square_sum = lax.psum(jnp.sum(gated_rows * gated_rows, axis=1, keepdims=True), "tp")
    inverse_gate = lax.rsqrt(square_sum / channel_total + EPSILON)
    unit_gate = gated_rows * inverse_gate
    mamba_rows = (unit_gate * gain_flat).astype(jnp.bfloat16)
    mixer_part = jnp.dot(attn_rows, w_attn_out, preferred_element_type=jnp.float32) + jnp.dot(
        mamba_rows, w_mamba_out, preferred_element_type=jnp.float32
    )
    mixer = lax.psum(mixer_part.astype(jnp.bfloat16), "tp").astype(jnp.float32)
    hidden = x_rows + mixer
    inverse_mid = lax.rsqrt(jnp.mean(hidden * hidden, axis=1, keepdims=True) + EPSILON)
    unit_mid = hidden * inverse_mid
    normed_mid = (unit_mid * norm_mid[None, :]).astype(jnp.bfloat16)
    gate_up = jnp.dot(
        normed_mid, w_gate_up.reshape(model_width, -1), preferred_element_type=jnp.float32
    ).reshape(rank_rows, 2, -1)
    gate_val = gate_up[:, 0]
    up_val = gate_up[:, 1]
    sigma = jax.nn.sigmoid(gate_val)
    activated = (gate_val * sigma * up_val).astype(jnp.bfloat16)
    ffn_part = jnp.dot(activated, w_down, preferred_element_type=jnp.float32)
    ffn_own = lax.psum_scatter(
        ffn_part.astype(jnp.bfloat16), "tp", scatter_dimension=0, tiled=True
    ).astype(jnp.float32)
    hidden_own = lax.dynamic_slice_in_dim(hidden, own_start, tok_rows, 0)
    out_own = (hidden_own + ffn_own).astype(jnp.bfloat16)
    grad_out = cot_rows.astype(jnp.float32)
    g_down = jnp.einsum("tf,td->fd", activated, cot_rows, preferred_element_type=jnp.float32)
    d_act = jnp.einsum("td,fd->tf", cot_rows, w_down, preferred_element_type=jnp.float32)
    d_gate = d_act * up_val * sigma * (1.0 + gate_val * (1.0 - sigma))
    d_up = d_act * gate_val * sigma
    d_gate_up = jnp.stack([d_gate, d_up], axis=1).astype(jnp.bfloat16)
    g_gate_up = jnp.einsum("td,tkf->dkf", normed_mid, d_gate_up, preferred_element_type=jnp.float32)
    d_mid_part = jnp.einsum("tkf,dkf->td", d_gate_up, w_gate_up, preferred_element_type=jnp.float32)
    d_mid = lax.psum(d_mid_part.astype(jnp.bfloat16), "tp").astype(jnp.float32)
    d_hidden = grad_out + norm_back(d_mid, unit_mid, inverse_mid, norm_mid)
    g_norm_mid = jnp.sum(lax.dynamic_slice_in_dim(d_mid * unit_mid, own_start, tok_rows, 0), axis=0)
    d_mix = d_hidden.astype(jnp.bfloat16)
    g_attn_out = jnp.einsum("tk,td->kd", attn_rows, d_mix, preferred_element_type=jnp.float32)
    g_mamba_out = jnp.einsum("tk,td->kd", mamba_rows, d_mix, preferred_element_type=jnp.float32)
    d_attn = jnp.einsum("td,kd->tk", d_mix, w_attn_out, preferred_element_type=jnp.float32).astype(
        jnp.bfloat16
    )
    d_mamba = jnp.einsum(
        "td,kd->tk", d_mix, w_mamba_out, preferred_element_type=jnp.float32
    ).astype(jnp.bfloat16)
    d_query_wide, d_keyval_wide = attn_pull(d_attn.astype(jnp.float32))
    d_query = d_query_wide.astype(jnp.bfloat16)
    d_keyval = d_keyval_wide.astype(jnp.bfloat16)
    d_mamba_wide = d_mamba.astype(jnp.float32)
    g_gain = jnp.sum(d_mamba_wide * unit_gate, axis=0).reshape(gain_mamba.shape)
    scaled_gate = d_mamba_wide * gain_flat
    gate_stat = lax.psum(jnp.sum(scaled_gate * unit_gate, axis=1, keepdims=True), "tp")
    d_gated = inverse_gate * (scaled_gate - unit_gate * (gate_stat / channel_total))
    d_gate_in, d_x_in, d_bc, d_step_wide, g_taps_x, g_taps_bc, g_heads = mamba_pull(d_gated)
    d_zx = jnp.stack([d_gate_in, d_x_in], axis=1).astype(jnp.bfloat16)
    d_step = d_step_wide.astype(jnp.bfloat16)
    g_query = jnp.einsum("td,tk->dk", normed_in, d_query, preferred_element_type=jnp.float32)
    g_keyval = jnp.einsum(
        "td,tk->dk", normed_in, d_keyval, preferred_element_type=jnp.float32
    ).reshape(w_keyval.shape)
    g_zx = jnp.einsum("td,tkc->dkc", normed_in, d_zx, preferred_element_type=jnp.float32)
    g_step = jnp.einsum("td,tk->dk", normed_in, d_step, preferred_element_type=jnp.float32)
    normed_wide = normed_in.astype(jnp.float32)
    g_bc = product(normed_wide.T, d_bc)
    d_in_part = jnp.einsum("tk,dk->td", d_query, w_query, preferred_element_type=jnp.float32)
    d_in_part = d_in_part + jnp.einsum(
        "tk,dk->td", d_keyval, w_keyval.reshape(model_width, -1), preferred_element_type=jnp.float32
    )
    d_in_part = d_in_part + jnp.einsum(
        "tkc,dkc->td", d_zx, w_zx, preferred_element_type=jnp.float32
    )
    d_in_part = d_in_part + jnp.einsum(
        "tk,dk->td", d_step, w_step, preferred_element_type=jnp.float32
    )
    d_in_part = d_in_part + product(d_bc, w_bc.astype(jnp.float32).T)
    d_in = lax.psum(d_in_part.astype(jnp.bfloat16), "tp").astype(jnp.float32)
    grad_x = d_hidden + norm_back(d_in, unit_in, inverse_in, norm_in)
    g_norm_in = jnp.sum(lax.dynamic_slice_in_dim(d_in * unit_in, own_start, tok_rows, 0), axis=0)
    grad_own = lax.dynamic_slice_in_dim(grad_x, own_start, tok_rows, 0).astype(jnp.bfloat16)
    own_sources = lax.dynamic_slice_in_dim(sources, own_start, tok_rows, 0)
    group_rows = gathered_tok.shape[0]
    out_buffer = (
        jnp.zeros((group_rows, model_width), jnp.float32)
        .at[own_sources]
        .set(out_own.astype(jnp.float32))
    )
    grad_buffer = (
        jnp.zeros((group_rows, model_width), jnp.float32)
        .at[own_sources]
        .set(grad_own.astype(jnp.float32))
    )
    mixed_home, grad_home = (
        lax.psum_scatter(
            out_buffer.astype(jnp.bfloat16), ("ctx", "tp"), scatter_dimension=0, tiled=True
        ).astype(jnp.float32),
        lax.psum_scatter(
            grad_buffer.astype(jnp.bfloat16), ("ctx", "tp"), scatter_dimension=0, tiled=True
        ).astype(jnp.float32),
    )
    head_cols = g_heads.shape[1]
    wide_heads = lax.dynamic_update_slice_in_dim(
        jnp.zeros((g_heads.shape[0], head_cols * tp_size), jnp.float32),
        g_heads,
        tp_index * head_cols,
        1,
    )
    wide_taps = lax.dynamic_update_slice_in_dim(
        jnp.zeros((g_taps_x.shape[0], head_cols * tp_size, g_taps_x.shape[2]), jnp.float32),
        g_taps_x,
        tp_index * head_cols,
        1,
    )
    wide_gain = lax.dynamic_update_slice_in_dim(
        jnp.zeros((head_cols * tp_size, g_gain.shape[1]), jnp.float32),
        g_gain,
        tp_index * head_cols,
        0,
    )
    sum_norm_in, sum_norm_mid, sum_heads, sum_bc, sum_taps_bc, sum_taps_x, sum_gain = lax.psum(
        (g_norm_in, g_norm_mid, wide_heads, g_bc, g_taps_bc, wide_taps, wide_gain),
        ("fsdp", "ctx", "tp"),
    )

    def shard_of(array, dim_index):
        piece = array.shape[dim_index] // fsdp_size
        return lax.dynamic_slice_in_dim(array, fsdp_index * piece, piece, dim_index)

    grad_norm_in = shard_of(sum_norm_in, 0)
    grad_norm_mid = shard_of(sum_norm_mid, 0)
    grad_heads = lax.dynamic_slice_in_dim(sum_heads, tp_index * head_cols, head_cols, 1)
    grad_bc = shard_of(sum_bc, 0)
    grad_taps_bc = shard_of(sum_taps_bc, 1)
    grad_taps_x = shard_of(
        lax.dynamic_slice_in_dim(sum_taps_x, tp_index * head_cols, head_cols, 1), 2
    )
    grad_gain = shard_of(lax.dynamic_slice_in_dim(sum_gain, tp_index * head_cols, head_cols, 0), 1)
    large_grads = (g_query, g_keyval, g_attn_out, g_zx, g_step, g_mamba_out, g_gate_up, g_down)
    wide_parts = (
        lax.psum_scatter(
            large_grads[0].astype(jnp.bfloat16), "fsdp", scatter_dimension=0, tiled=True
        ).astype(jnp.float32),
        lax.psum_scatter(
            large_grads[1].astype(jnp.bfloat16), "fsdp", scatter_dimension=0, tiled=True
        ).astype(jnp.float32),
        lax.psum_scatter(
            large_grads[2].astype(jnp.bfloat16), "fsdp", scatter_dimension=1, tiled=True
        ).astype(jnp.float32),
        lax.psum_scatter(
            large_grads[3].astype(jnp.bfloat16), "fsdp", scatter_dimension=0, tiled=True
        ).astype(jnp.float32),
        lax.psum_scatter(
            large_grads[4].astype(jnp.bfloat16), "fsdp", scatter_dimension=0, tiled=True
        ).astype(jnp.float32),
        lax.psum_scatter(
            large_grads[5].astype(jnp.bfloat16), "fsdp", scatter_dimension=1, tiled=True
        ).astype(jnp.float32),
        lax.psum_scatter(
            large_grads[6].astype(jnp.bfloat16), "fsdp", scatter_dimension=0, tiled=True
        ).astype(jnp.float32),
        lax.psum_scatter(
            large_grads[7].astype(jnp.bfloat16), "fsdp", scatter_dimension=1, tiled=True
        ).astype(jnp.float32),
    )
    reduced = (
        lax.psum(wide_parts[0].astype(jnp.bfloat16), "ctx").astype(jnp.float32),
        lax.psum(wide_parts[1].astype(jnp.bfloat16), "ctx").astype(jnp.float32),
        lax.psum(wide_parts[2].astype(jnp.bfloat16), "ctx").astype(jnp.float32),
        lax.psum(wide_parts[3].astype(jnp.bfloat16), "ctx").astype(jnp.float32),
        lax.psum(wide_parts[4].astype(jnp.bfloat16), "ctx").astype(jnp.float32),
        lax.psum(wide_parts[5].astype(jnp.bfloat16), "ctx").astype(jnp.float32),
        lax.psum(wide_parts[6].astype(jnp.bfloat16), "ctx").astype(jnp.float32),
        lax.psum(wide_parts[7].astype(jnp.bfloat16), "ctx").astype(jnp.float32),
    )
    (
        grad_query,
        grad_keyval,
        grad_attn_out,
        grad_zx,
        grad_step,
        grad_mamba_out,
        grad_gate_up,
        grad_down,
    ) = reduced
    return (
        mixed_home.astype(jnp.bfloat16),
        grad_home.astype(jnp.bfloat16),
        grad_norm_in,
        grad_query,
        grad_keyval,
        grad_attn_out,
        grad_zx,
        grad_bc,
        grad_step,
        grad_heads,
        grad_taps_x,
        grad_taps_bc,
        grad_gain,
        grad_mamba_out,
        grad_norm_mid,
        grad_gate_up,
        grad_down,
    )


def solution(mesh):
    in_specs = (
        P(("fsdp", "ctx", "tp"), None),
        P(("fsdp", "ctx", "tp"), None),
        P("fsdp", None),
        P("fsdp", None),
        P("fsdp"),
        P("fsdp", "tp"),
        P("fsdp", "tp", None),
        P("tp", "fsdp"),
        P("fsdp", None, "tp"),
        P("fsdp", None),
        P("fsdp", "tp"),
        P(None, "tp"),
        P(None, "tp", "fsdp"),
        P(None, "fsdp"),
        P("tp", "fsdp"),
        P("tp", "fsdp"),
        P("fsdp"),
        P("fsdp", None, "tp"),
        P("tp", "fsdp"),
    )
    out_specs = (
        P(("fsdp", "ctx", "tp"), None),
        P(("fsdp", "ctx", "tp"), None),
        P("fsdp"),
        P("fsdp", "tp"),
        P("fsdp", "tp", None),
        P("tp", "fsdp"),
        P("fsdp", None, "tp"),
        P("fsdp", None),
        P("fsdp", "tp"),
        P(None, "tp"),
        P(None, "tp", "fsdp"),
        P(None, "fsdp"),
        P("tp", "fsdp"),
        P("tp", "fsdp"),
        P("fsdp"),
        P("fsdp", None, "tp"),
        P("tp", "fsdp"),
    )
    return jax.shard_map(
        per_device, mesh=mesh, in_specs=in_specs, out_specs=out_specs, check_vma=False
    )
```

profile of v0, /device:TPU:0, one launch (start us, length us, event | category | flops | bytes accessed | tf_op | source)
XLA Modules:
  0.0 1255.0 jit_solution(17165648265060494013)
XLA Ops:
  14.4 12.6 %all-gather = bf16[4,1,256]{2,1,0:T(2,128)(2,1)S(1)} all-gather(bf16[1,1,256]{2,1,0:T(2,128)(2,1)S(1)} %reshape.1312), channel_id=1, replica_groups=mesh['fsdp'=4,'ctx'=4,'tp'=2] {'fsdp'}, dimensions={0}, use_global_device_ids=true | all-gather | bytes 2560 | tf_op jit(solution)/shard_map/all_gather | solution.py:263
  28.5 12.1 all-gather.1
  41.3 13.4 %all_gather.58 = bf16[12,64]{0,1:T(8,128)(2,1)S(1)} all-gather(bf16[12,16]{0,1:T(8,128)(2,1)S(1)} %copy.301), channel_id=1, replica_groups=mesh['fsdp'=4,'ctx'=4,'tp'=2] {'fsdp'}, dimensions={1}, use_global_device_ids=true | all-gather | bytes 1920 | tf_op jit(solution)/shard_map/all_gather | solution.py:272
  55.5 14.1 %all_gather.53 = bf16[1024,12]{0,1:T(8,128)(2,1)} all-gather(bf16[256,12]{0,1:T(8,128)(2,1)S(1)} %copy-done.152), channel_id=1, replica_groups=mesh['fsdp'=4,'ctx'=4,'tp'=2] {'fsdp'}, dimensions={0}, use_global_device_ids=true | all-gather | bytes 30720 | tf_op jit(solution)/shard_map/all_gather | solution.py:269
  69.7 13.9 %all_gather.54 = bf16[5,12,64]{1,0,2:T(8,128)(2,1)S(1)} all-gather(bf16[5,12,16]{1,0,2:T(8,128)(2,1)S(1)} %copy.287), channel_id=1, replica_groups=mesh['fsdp'=4,'ctx'=4,'tp'=2] {'fsdp'}, dimensions={2}, use_global_device_ids=true | all-gather | bytes 9600 | tf_op jit(solution)/shard_map/all_gather | solution.py:270
  87.5 14.5 %all_gather.50 = bf16[1024,1,128]{2,0,1:T(8,128)(2,1)S(1)} all-gather(bf16[256,1,128]{2,0,1:T(8,128)(2,1)S(1)} %copy-done.90), channel_id=1, replica_groups=mesh['fsdp'=4,'ctx'=4,'tp'=2] {'fsdp'}, dimensions={0}, use_global_device_ids=true | all-gather | bytes 327680 | tf_op jit(solution)/shard_map/all_gather | solution.py:265
  101.9 16.3 %all_gather.51 = bf16[1024,256]{1,0:T(8,128)(2,1)} all-gather(bf16[256,256]{1,0:T(8,128)(2,1)S(1)} %copy-done.81), channel_id=1, replica_groups=mesh['fsdp'=4,'ctx'=4,'tp'=2] {'fsdp'}, dimensions={0}, use_global_device_ids=true | all-gather | bytes 655360 | tf_op jit(solution)/shard_map/all_gather | solution.py:264
  118.2 18.7 %all_gather.52 = bf16[256,1024]{1,0:T(8,128)(2,1)} all-gather(bf16[256,256]{1,0:T(8,128)(2,1)S(1)} %copy-done.82), channel_id=1, replica_groups=mesh['fsdp'=4,'ctx'=4,'tp'=2] {'fsdp'}, dimensions={1}, use_global_device_ids=true | all-gather | bytes 655360 | tf_op jit(solution)/shard_map/all_gather | solution.py:266
  137.0 19.9 %all_gather.57 = bf16[1024,256]{1,0:T(8,128)(2,1)S(1)} all-gather(bf16[256,256]{1,0:T(8,128)(2,1)S(1)} %copy-done.83), channel_id=1, replica_groups=mesh['fsdp'=4,'ctx'=4,'tp'=2] {'fsdp'}, dimensions={0}, use_global_device_ids=true | all-gather | bytes 655360 | tf_op jit(solution)/shard_map/all_gather | solution.py:268
  158.8 4.9 copy.291
  163.8 5.5 gather_fusion
  199.7 86.1 %while.46 = (s32[]{:T(128)}, f32[12,64,128]{2,1,0:T(8,128)S(1)}, s32[]{:T(128)}, f32[4,128,12,64]{1,0,3,2:T(4,128)}, f32[4,12,64,128]{3,2,1,0:T(8,128)}, /*index...) while((s32[]{:T(128)}, f32[12,64,128]{2,1,0:T(8,128)S(1)}, ...), condition=%wide.region_14.16_spmd.clone, body=%wide.region_12.15_spmd.clone.sunk | while | flops 480172544 | bytes 5295634 | solution.py:190
  208.0 10.7 dynamic_update_slice.90
  229.4 10.7 dynamic_update_slice.90
  250.8 10.7 dynamic_update_slice.90
  272.2 10.7 dynamic_update_slice.90
  295.9 5.1 psum.140
  309.0 8.2 all-gather.2
  317.2 6.4 copy.304
  323.7 6.2 gather_fusion.1
  329.9 17.7 %all-reduce.45.cloned.1.call-done = bf16[512,1024]{1,0:T(8,128)(2,1)} async-done(((bf16[512,1024]{1,0:T(8,128)(2,1)}), bf16[512,1024]{1,0:T(8,128)(2,1)}) %all-reduce.45.cloned.1.call-update) | async-done | bytes 1048592 | tf_op jit(solution)/shard_map/psum | solution.py:327
  357.8 37.7 %all-gather.18.cloned.1.call-done = bf16[1024,1024]{1,0:T(8,128)(2,1)} async-done(((bf16[1024,256]{1,0:T(8,128)(2,1)}), bf16[1024,1024]{1,0:T(8,128)(2,1)}) %all-gather.18.cloned.1.call-update) | async-done | bytes 2097168 | tf_op jit(solution)/shard_map/all_gather | solution.py:276
  395.5 6.3 fusion.158
  409.2 35.7 %all-reduce.47.cloned.1.call-done = bf16[512,1024]{1,0:T(8,128)(2,1)} async-done(((bf16[512,1024]{1,0:T(8,128)(2,1)}), bf16[512,1024]{1,0:T(8,128)(2,1)}) %all-reduce.47.cloned.1.call-update) | async-done | bytes 1048592 | tf_op jit(solution)/shard_map/psum | solution.py:353
  485.1 5.0 fusion.107
  490.1 4.9 psum.143
  495.0 5.4 multiply_reduce_fusion.12
  513.4 174.2 %while.47 = (s32[]{:T(128)}, f32[12]{0:T(128)}, f32[12,64,128]{2,1,0:T(8,128)}, f32[4,128,12,64]{1,0,3,2:T(4,128)}, f32[4,128,128]{2,1,0:T(8,128)}, /*index=5*/f...) while((s32[]{:T(128)}, f32[12]{0:T(128)}, ...), condition=%wide.region_48.50_spmd.clone, body=%wide.region_36.49_spmd.clone.sunk | while | flops 1138265088 | bytes 13988434 | solution.py:190
  545.0 10.7 dynamic_update_slice.95
  588.9 10.7 dynamic_update_slice.95
  632.8 10.7 dynamic_update_slice.95
  676.7 10.7 dynamic_update_slice.95
  706.8 5.9 convolution_convert_fusion
  730.5 35.0 %reduce-scatter.24.cloned.1.call-done = bf16[256,2,768]{2,0,1:T(8,128)(2,1)} async-done(((bf16[1024,2,768]{2,0,1:T(8,128)(2,1)}), bf16[256,2,768]{2,0,1:T(8,128)(2,1)}) %reduce-scatter.24.cloned.1.call-update) | async-done | bytes 786448 | tf_op jit(solution)/shard_map/reduce_scatter | solution.py:467
  765.6 79.0 %reduce-scatter.30.cloned.1.call-done = bf16[256,2,1024]{2,0,1:T(8,128)(2,1)} async-done(((bf16[1024,2,1024]{2,0,1:T(8,128)(2,1)}), bf16[256,2,1024]{2,0,1:T(8,128)(2,1)}) %reduce-scatter.30.cloned.1.call-update) | async-done | bytes 1048592 | tf_op jit(solution)/shard_map/reduce_scatter | solution.py:476
  844.8 43.2 %all-reduce.49.cloned.1.call-done = bf16[512,1024]{1,0:T(8,128)(2,1)} async-done(((bf16[512,1024]{1,0:T(8,128)(2,1)}), bf16[512,1024]{1,0:T(8,128)(2,1)}) %all-reduce.49.cloned.1.call-update) | async-done | bytes 1048592 | tf_op jit(solution)/shard_map/psum | solution.py:395
  891.3 6.6 scatter_custom_fusion.1
  897.9 6.1 convert_element_type.395
  904.2 6.8 reduce-scatter.12.cloned.1.call-done
  911.0 5.8 scatter_custom_fusion
  916.8 6.0 convert_element_type.366
  925.6 7.1 reduce-scatter.26.cloned.1.call-done
  932.7 5.9 psum.151
  939.2 126.7 %all-reduce.51.cloned.1.call-done = f32[1024,256]{1,0:T(8,128)} async-done(((f32[1024,256]{1,0:T(8,128)}), f32[1024,256]{1,0:T(8,128)}) %all-reduce.51.cloned.1.call-update) | async-done | bytes 1048592 | tf_op jit(solution)/shard_map/psum | solution.py:438
  1067.9 41.1 %all-reduce.37 = (f32[1024]{0:T(1024)S(1)}, f32[3,24]{1,0:T(4,128)S(1)}, f32[5,24,64]{2,1,0:T(8,128)S(1)}, f32[5,256]{1,0:T(8,128)S(1)}, f32[24,64]{1,0:T(8,128)S(1)}, /*index=5*/f32[1024]{0:T(1024)S(1)}) all-reduce(f32[1024]{0:T(1024)S(1)} %fusion.142, ...), channel_id=1, replica_groups=mesh['fsdp'=4,'ctx'=4,'tp'=2] {'fsdp','ctx','tp'}, use_global_device_ids=true, to_apply=%region_54.56 | all-reduce | flops 12616 | bytes 100928 | tf_op jit(solution)/shard_map/psum | solution.py:438
  1113.0 23.7 %all-reduce.53.cloned.1.call-done = (bf16[256,2,768]{2,0,1:T(8,128)(2,1)}, bf16[256,2,1024]{2,0,1:T(8,128)(2,1)}, bf16[256,256]{1,0:T(8,128)(2,1)}, bf16[256,1,1...) async-done(((bf16[256,2,768]{2,0,1:T(8,128)(2,1)}, bf16[256,2,1024]{2,0,1:T(8,128)(2,1)}, ...) | async-done | bytes 3080208 | tf_op jit(solution)/shard_map/psum | solution.py:487
  1149.2 43.1 %reduce-scatter.16.cloned.1.call-done = bf16[256,1024]{1,0:T(8,128)(2,1)} async-done(((bf16[2048,1024]{1,0:T(8,128)(2,1)}), bf16[256,1024]{1,0:T(8,128)(2,1)}) %reduce-scatter.16.cloned.1.call-update) | async-done | bytes 524304 | tf_op jit(solution)/shard_map/reduce_scatter | solution.py:415
  1192.3 55.7 %reduce-scatter.14.cloned.1.call-done = bf16[256,1024]{1,0:T(8,128)(2,1)} async-done(((bf16[2048,1024]{1,0:T(8,128)(2,1)}), bf16[256,1024]{1,0:T(8,128)(2,1)}) %reduce-scatter.14.cloned.1.call-update) | async-done | bytes 524304 | tf_op jit(solution)/shard_map/reduce_scatter | solution.py:412
  (927 shorter events, 358.7 us)
Async XLA Ops:
  7.2 151.6 %all-gather.12.cloned.1.call-start = ((), (), s32[]{:S(2)}) async-start(), calls=%async_computation.12 | async-start | bytes 3932160 | tf_op jit(solution)/shard_map/all_gather | solution.py:267
  9.4 154.3 %all-gather.10.cloned.1.call-start = ((), (), s32[]{:S(2)}) async-start(), calls=%async_computation.11 | async-start | bytes 4718592 | tf_op jit(solution)/shard_map/all_gather | solution.py:244
  10.3 293.8 %all-gather.14.cloned.1.call-start = ((), (), s32[]{:S(2)}) async-start(), calls=%async_computation.13 | async-start | bytes 1966080 | tf_op jit(solution)/shard_map/all_gather | solution.py:273
  11.0 76.4 %copy-start.90 = (bf16[256,1,128]{2,0,1:T(8,128)(2,1)S(1)}, bf16[256,1,128]{2,0,1:T(8,128)(2,1)}, u32[]{:S(2)}) copy-start(bf16[256,1,128]{2,0,1:T(8,128)(2,1)} %param.31) | copy-start | bytes 196612
  11.0 90.9 %copy-start.81 = (bf16[256,256]{1,0:T(8,128)(2,1)S(1)}, bf16[256,256]{1,0:T(8,128)(2,1)}, u32[]{:S(2)}) copy-start(bf16[256,256]{1,0:T(8,128)(2,1)} %param.30) | copy-start | bytes 393220
  11.0 306.2 %all-gather.16.cloned.1.call-start = ((), (), s32[]{:S(2)}) async-start(), calls=%async_computation.15 | async-start | bytes 5242880 | tf_op jit(solution)/shard_map/all_gather | solution.py:275
  12.4 105.9 %copy-start.82 = (bf16[256,256]{1,0:T(8,128)(2,1)S(1)}, bf16[256,256]{1,0:T(8,128)(2,1)}, u32[]{:S(2)}) copy-start(bf16[256,256]{1,0:T(8,128)(2,1)} %param.32) | copy-start | bytes 393220
  12.4 124.6 %copy-start.83 = (bf16[256,256]{1,0:T(8,128)(2,1)S(1)}, bf16[256,256]{1,0:T(8,128)(2,1)}, u32[]{:S(2)}) copy-start(bf16[256,256]{1,0:T(8,128)(2,1)} %param.34) | copy-start | bytes 393220
  12.4 311.3 %all-gather.20.cloned.1.call-start = ((), (), s32[]{:S(2)}) async-start(), calls=%async_computation.19 | async-start | bytes 4718592 | tf_op jit(solution)/shard_map/all_gather | solution.py:245
  13.0 334.6 %all-reduce.45.cloned.1.call-start = ((), (), s32[]{:S(2)}) async-start(), calls=%async_computation.14 | async-start | bytes 2097152 | tf_op jit(solution)/shard_map/psum | solution.py:327
  13.0 150.7 %copy-start.153 = (f32[32]{0:T(128)}, f32[32]{0:T(128)S(1)}, u32[]{:S(2)}) copy-start(f32[32]{0:T(128)S(1)} %multiply_power_fusion) | copy-start | bytes 388
  14.2 149.5 %copy-start.144 = (s32[256]{0:T(256)}, s32[256]{0:T(256)S(1)}, u32[]{:S(2)}) copy-start(s32[256]{0:T(256)S(1)} %slice.189) | copy-start | bytes 3076
  14.3 149.5 %copy-start.146 = (s32[256]{0:T(256)}, s32[256]{0:T(256)S(1)}, u32[]{:S(2)}) copy-start(s32[256]{0:T(256)S(1)} %slice.182) | copy-start | bytes 3076
  14.4 149.4 %copy-start.114 = (f32[512]{0:T(512)}, f32[512]{0:T(512)S(1)}, u32[]{:S(2)}) copy-start(f32[512]{0:T(512)S(1)} %fusion.234) | copy-start | bytes 6148
  14.4 149.3 %copy-start.148 = (s32[256]{0:T(256)}, s32[256]{0:T(256)S(1)}, u32[]{:S(2)}) copy-start(s32[256]{0:T(256)S(1)} %get-tuple-element.508) | copy-start | bytes 3076
  14.4 149.3 %copy-start.150 = (s32[256]{0:T(256)}, s32[256]{0:T(256)S(1)}, u32[]{:S(2)}) copy-start(s32[256]{0:T(256)S(1)} %get-tuple-element.516) | copy-start | bytes 3076
  27.1 142.7 %copy-start.109 = (f32[4,1,256]{2,1,0:T(1,128)}, f32[4,1,256]{2,1,0:T(1,128)S(1)}, u32[]{:S(2)}) copy-start(f32[4,1,256]{2,1,0:T(1,128)S(1)} %convert_element_type.413) | copy-start | bytes 12292
  27.7 142.0 %copy-start.122 = (pred[512]{0:T(512)(128)(4,1)}, pred[512]{0:T(512)(128)(4,1)S(1)}, u32[]{:S(2)}) copy-start(pred[512]{0:T(512)(128)(4,1)S(1)} %get-tuple-element.1093) | copy-start | bytes 1540
  27.8 161.6 %copy-start.95 = (f32[512]{0:T(512)}, f32[512]{0:T(512)S(1)}, u32[]{:S(2)}) copy-start(f32[512]{0:T(512)S(1)} %get-tuple-element.1092) | copy-start | bytes 6148
  27.8 161.6 %copy-start.97 = (f32[512]{0:T(512)}, f32[512]{0:T(512)S(1)}, u32[]{:S(2)}) copy-start(f32[512]{0:T(512)S(1)} %get-tuple-element.1090) | copy-start | bytes 6148
  28.3 135.5 %copy-start.130 = (s32[1024]{0:T(1024)}, s32[1024]{0:T(1024)S(1)}, u32[]{:S(2)}) copy-start(s32[1024]{0:T(1024)S(1)} %pad_clamp_fusion) | copy-start | bytes 12292
  28.5 466.5 %copy-start.91 = (f32[768]{0:T(1024)}, f32[768]{0:T(1024)S(1)}, u32[]{:S(2)}) copy-start(f32[768]{0:T(1024)S(1)} %mul.1456) | copy-start | bytes 9220
  101.9 68.8 %copy-start.44 = (bf16[1024,1,128]{2,0,1:T(8,128)(2,1)}, bf16[1024,1,128]{2,0,1:T(8,128)(2,1)S(1)}, u32[]{:S(2)}) copy-start(bf16[1024,1,128]{2,0,1:T(8,128)(2,1)S(1)} %all_gather.50) | copy-start | bytes 786436
  308.2 87.3 %all-gather.18.cloned.1.call-start = ((), (), s32[]{:S(2)}) async-start(), calls=%async_computation.16 | async-start | bytes 2621440 | tf_op jit(solution)/shard_map/all_gather | solution.py:276
  308.9 136.0 %all-reduce.47.cloned.1.call-start = ((), (), s32[]{:S(2)}) async-start(), calls=%async_computation.20 | async-start | bytes 2097152 | tf_op jit(solution)/shard_map/psum | solution.py:353
  317.2 129.6 %copy-start.111 = (f32[4,1,256]{2,1,0:T(1,128)}, f32[4,1,256]{2,1,0:T(1,128)S(1)}, u32[]{:S(2)}) copy-start(f32[4,1,256]{2,1,0:T(1,128)S(1)} %convert_element_type.415) | copy-start | bytes 12292
  349.7 97.1 %copy-start = (f32[512,1024]{1,0:T(8,128)}, f32[512,1024]{1,0:T(8,128)S(1)}, u32[]{:S(2)}) copy-start(f32[512,1024]{1,0:T(8,128)S(1)} %get-tuple-element.1016) | copy-start | bytes 6291460
  406.5 323.9 %reduce-scatter.20.cloned.1.call-start = ((), (), s32[]{:S(2)}) async-start(), calls=%async_computation.24 | async-start | bytes 327680 | tf_op jit(solution)/shard_map/reduce_scatter | solution.py:461
  473.3 257.2 %reduce-scatter.22.cloned.1.call-start = ((), (), s32[]{:S(2)}) async-start(), calls=%async_computation.25 | async-start | bytes 655360 | tf_op jit(solution)/shard_map/reduce_scatter | solution.py:464
  474.6 255.8 %reduce-scatter.18.cloned.1.call-start = ((), (), s32[]{:S(2)}) async-start(), calls=%async_computation.23 | async-start | bytes 655360 | tf_op jit(solution)/shard_map/reduce_scatter | solution.py:458
  481.3 249.2 %reduce-scatter.32.cloned.1.call-start = ((), (), s32[]{:S(2)}) async-start(), calls=%async_computation.31 | async-start | bytes 2621440 | tf_op jit(solution)/shard_map/reduce_scatter | solution.py:479
  484.3 246.2 %reduce-scatter.28.cloned.1.call-start = ((), (), s32[]{:S(2)}) async-start(), calls=%async_computation.29 | async-start | bytes 1966080 | tf_op jit(solution)/shard_map/reduce_scatter | solution.py:473
  509.8 255.8 %reduce-scatter.24.cloned.1.call-start = ((), (), s32[]{:S(2)}) async-start(), calls=%async_computation.26 | async-start | bytes 3932160 | tf_op jit(solution)/shard_map/reduce_scatter | solution.py:467
  705.2 139.3 %reduce-scatter.30.cloned.1.call-start = ((), (), s32[]{:S(2)}) async-start(), calls=%async_computation.30 | async-start | bytes 5242880 | tf_op jit(solution)/shard_map/reduce_scatter | solution.py:476
  712.8 175.2 %all-reduce.49.cloned.1.call-start = ((), (), s32[]{:S(2)}) async-start(), calls=%async_computation.21 | async-start | bytes 2097152 | tf_op jit(solution)/shard_map/psum | solution.py:395
  723.2 187.8 %reduce-scatter.12.cloned.1.call-start = ((), (), s32[]{:S(2)}) async-start(), calls=%async_computation.17 | async-start | bytes 1572864 | tf_op jit(solution)/shard_map/reduce_scatter | solution.py:340
  727.1 205.6 %reduce-scatter.26.cloned.1.call-start = ((), (), s32[]{:S(2)}) async-start(), calls=%async_computation.28 | async-start | bytes 40960 | tf_op jit(solution)/shard_map/reduce_scatter | solution.py:470
  728.0 337.8 %all-reduce.51.cloned.1.call-start = ((), (), s32[]{:S(2)}) async-start(), calls=%async_computation.27 | async-start | bytes 2097152 | tf_op jit(solution)/shard_map/psum | solution.py:438
  730.3 114.3 %copy-start.134 = (s32[512]{0:T(512)S(1)}, s32[512]{0:T(512)}, u32[]{:S(2)}) copy-start(s32[512]{0:T(512)} %copy-done.133) | copy-start | bytes 6148
  730.3 114.4 %copy-start.119 = (f32[512]{0:T(512)S(1)}, f32[512]{0:T(512)}, u32[]{:S(2)}) copy-start(f32[512]{0:T(512)} %copy-done.118) | copy-start | bytes 6148
  730.3 157.6 %copy-start.8 = (bf16[512,1024]{1,0:T(8,128)(2,1)S(1)}, bf16[512,1024]{1,0:T(8,128)(2,1)}, u32[]{:S(2)}) copy-start(bf16[512,1024]{1,0:T(8,128)(2,1)} %copy-done.7) | copy-start | bytes 3145732
  730.3 157.6 %copy-start.110 = (f32[4,1,256]{2,1,0:T(1,128)S(1)}, f32[4,1,256]{2,1,0:T(1,128)}, u32[]{:S(2)}) copy-start(f32[4,1,256]{2,1,0:T(1,128)} %copy-done.109) | copy-start | bytes 12292
  730.3 157.6 %copy-start.125 = (pred[512]{0:T(512)(128)(4,1)S(1)}, pred[512]{0:T(512)(128)(4,1)}, u32[]{:S(2)}) copy-start(pred[512]{0:T(512)(128)(4,1)} %copy-done.122) | copy-start | bytes 1540
  730.4 406.4 %all-reduce.53.cloned.1.call-start = ((), (), s32[]{:S(2)}) async-start(), calls=%async_computation.32 | async-start | bytes 6160384 | tf_op jit(solution)/shard_map/psum | solution.py:487
  844.6 347.7 %reduce-scatter.16.cloned.1.call-start = ((), (), s32[]{:S(2)}) async-start(), calls=%async_computation.22 | async-start | bytes 4718592 | tf_op jit(solution)/shard_map/reduce_scatter | solution.py:415
  904.0 344.0 %reduce-scatter.14.cloned.1.call-start = ((), (), s32[]{:S(2)}) async-start(), calls=%async_computation.18 | async-start | bytes 4718592 | tf_op jit(solution)/shard_map/reduce_scatter | solution.py:412
  925.4 142.1 %copy-start.37 = (bf16[512,1024]{1,0:T(8,128)(2,1)S(1)}, bf16[512,1024]{1,0:T(8,128)(2,1)}, u32[]{:S(2)}) copy-start(bf16[512,1024]{1,0:T(8,128)(2,1)} %all-reduce.49.cloned.1.call-done) | copy-start | bytes 3145732
  925.6 142.2 %copy-start.26 = (f32[512,1024]{1,0:T(8,128)S(1)}, f32[512,1024]{1,0:T(8,128)}, u32[]{:S(2)}) copy-start(f32[512,1024]{1,0:T(8,128)} %copy-done.25) | copy-start | bytes 6291460
  (181 other events, 901.4 us)
Sparse Core Ops, SparseCore 0:
  10.2 68.5 all-gather.11
  80.7 35.4 all-gather.9
  117.7 45.5 all-gather.13
  165.3 78.9 all-gather.15
  246.0 35.2 all-gather.19
  308.3 39.2 all-reduce.44
  349.2 46.2 all-gather.17
  406.6 38.2 all-reduce.46
  473.4 19.5 reduce-scatter.19
  495.3 19.9 reduce-scatter.21
  517.7 19.9 reduce-scatter.17
  539.9 42.1 reduce-scatter.31
  584.4 34.2 reduce-scatter.27
  705.3 60.2 reduce-scatter.23
  767.7 76.7 reduce-scatter.29
  847.4 40.5 all-reduce.48
  890.6 20.3 reduce-scatter.11
  913.7 18.9 reduce-scatter.25
  937.9 127.9 all-reduce.50
  1068.8 67.8 all-reduce.52
  1140.7 51.5 reduce-scatter.15
  1196.6 51.3 reduce-scatter.13
where the time goes:
time: 1260 us
  waiting for transfers between devices  514 us (41%)
  local copies, waits for them, and re-layouts  226 us (18%)
  blocking collectives  201 us (16%)
  matrix products  147 us (12%)
  other arithmetic  137 us (11%)
  between operations  16.7 us (1%)
    psum x1, waiting for transfers between devices, per_device(): lax.psum((g_norm_in, g_norm_mid, wide_heads, g_bc, g_taps_bc, wide_taps,...  127 us
    dynamic_update_slice x12, local copies, waits for them, and re-layouts, state_space(): final_carry, outputs = lax.scan(jax.checkpoint(advance), start, pieces)  85.9 us
    reduce_scatter x1, waiting for transfers between devices, per_device(): lax.psum_scatter(large_grads[6].astype(jnp.bfloat16), 'fsdp', scatter_dim...  79 us
    reduce_scatter x1, waiting for transfers between devices, per_device(): lax.psum_scatter(out_buffer.astype(jnp.bfloat16), ('ctx', 'tp'), scatter_...  55.7 us
    psum x1, waiting for transfers between devices, per_device(): d_in = lax.psum(d_in_part.astype(jnp.bfloat16), 'tp').astype(jnp.float32)  43.2 us
    reduce_scatter x1, waiting for transfers between devices, per_device(): lax.psum_scatter(grad_buffer.astype(jnp.bfloat16), ('ctx', 'tp'), scatter...  43.1 us
    psum x1, blocking collectives, per_device(): lax.psum((g_norm_in, g_norm_mid, wide_heads, g_bc, g_taps_bc, wide_taps,...  41.1 us
    all_gather x1, waiting for transfers between devices, per_device(): lax.all_gather(w_down, 'fsdp', axis=1, tiled=True)  37.7 us
  transfers between devices with their start and end apart: 22, of which 12 were waited for; matrix products, arithmetic and copies ran while one was open for 36% of the time, Pallas kernels for 0%

commit v1 on v0

v1 whole, which is shorter than its diff:
```python
import jax
import jax.numpy as jnp
from jax import lax
from jax.experimental import pallas as pl
from jax.experimental.pallas import tpu as pltpu
from jax.sharding import PartitionSpec as P

HD = 64
BLK = 128
LANES = 128
EPSILON = 1e-05
ROPE_BASE = 100000000000.0
PRECISE = lax.Precision.HIGHEST
F32 = jnp.float32
BF = jnp.bfloat16
FAR = -1e30


def dot_nn(a, b, precision=None):
    return lax.dot_general(
        a, b, (((1,), (0,)), ((), ())), precision=precision, preferred_element_type=F32
    )


def dot_nt(a, b, precision=None):
    return lax.dot_general(
        a, b, (((1,), (1,)), ((), ())), precision=precision, preferred_element_type=F32
    )


def dot_tn(a, b, precision=None):
    return lax.dot_general(
        a, b, (((0,), (0,)), ((), ())), precision=precision, preferred_element_type=F32
    )


def iota(shape, dim):
    return lax.broadcasted_iota(jnp.int32, shape, dim)


def swap_halves(v):
    lanes = v.shape[1]
    low = (iota(v.shape, 1) & (HD - 1)) < HD // 2
    return jnp.where(low, pltpu.roll(v, lanes - HD // 2, 1), pltpu.roll(v, HD // 2, 1))


def split_pair(v):
    first = iota(v.shape, 1) < HD
    zero = jnp.zeros_like(v)
    return jnp.concatenate([jnp.where(first, v, zero), jnp.where(first, zero, v)], axis=0)


def keys_values(kv, cos, sin):
    first = iota(kv.shape, 1) < HD
    roped = kv * cos + swap_halves(kv) * sin
    keys = jnp.where(first, roped, 0.0)
    values = jnp.where(first, 0.0, kv)
    key_pair = (keys.astype(BF), pltpu.roll(keys, HD, 1).astype(BF))
    value_pair = (pltpu.roll(values, HD, 1).astype(BF), values.astype(BF))
    return key_pair, value_pair


def attention_probs(query, key, allowed):
    scores = dot_nt(query, key) * HD ** (-0.5)
    scores = jnp.where(allowed, scores, FAR)
    weights = jnp.exp(scores - jnp.max(scores, axis=1, keepdims=True))
    return weights / jnp.sum(weights, axis=1, keepdims=True)


def allowed_rows(segc, segr, lower, count):
    keys = lower + count
    same = segc[lower:keys, :] == segr[:, :keys]
    return same & (iota((count, keys), 0) + lower >= iota((count, keys), 1))


def attention_fwd_kernel(q_ref, kv_ref, cos_ref, sin_ref, segc_ref, segr_ref, out_ref):
    rows, width = q_ref.shape
    cos, sin = cos_ref[...], sin_ref[...]
    key_pair, value_pair = keys_values(kv_ref[...], cos, sin)
    segc, segr = segc_ref[...], segr_ref[...]
    for pair in range(width // LANES):
        cols = slice(pair * LANES, (pair + 1) * LANES)
        raw = q_ref[:, cols]
        query = (raw * cos + swap_halves(raw) * sin).astype(BF)
        for lower in range(0, rows, BLK):
            keys = lower + BLK
            allowed = allowed_rows(segc, segr, lower, BLK)
            total = None
            for side in range(2):
                probs = attention_probs(query[lower:keys], key_pair[side][:keys], allowed)
                part = dot_nn(probs.astype(BF), value_pair[side][:keys])
                total = part if total is None else total + part
            out_ref[lower:keys, cols] = total.astype(BF)


def attention_bwd_kernel(
    q_ref, kv_ref, cos_ref, sin_ref, segc_ref, segr_ref, do_ref, out_ref, dk_ref, dv_ref
):
    rows, width = q_ref.shape
    cos, sin = cos_ref[...], sin_ref[...]
    key_pair, value_pair = keys_values(kv_ref[...], cos, sin)
    segc, segr = segc_ref[...], segr_ref[...]
    dk_ref[...] = jnp.zeros_like(dk_ref)
    dv_ref[...] = jnp.zeros_like(dv_ref)
    for pair in range(width // LANES):
        cols = slice(pair * LANES, (pair + 1) * LANES)
        raw = q_ref[:, cols]
        query = (raw * cos + swap_halves(raw) * sin).astype(BF)
        for lower in range(0, rows, BLK):
            keys = lower + BLK
            allowed = allowed_rows(segc, segr, lower, BLK)
            query_part = query[lower:keys]
            grad = do_ref[lower:keys, cols]
            d_query = None
            probs_all, scores_all = [], []
            for side in range(2):
                probs = attention_probs(query_part, key_pair[side][:keys], allowed)
                d_probs = dot_nt(grad, value_pair[side][:keys])
                inner = jnp.sum(d_probs * probs, axis=1, keepdims=True)
                d_scores = (probs * (d_probs - inner)).astype(BF)
                part = dot_nn(d_scores, key_pair[side][:keys])
                d_query = part if d_query is None else d_query + part
                probs_all.append(probs.astype(BF))
                scores_all.append(d_scores)
            dv_ref[:keys, :] += dot_tn(jnp.concatenate(probs_all, axis=0), split_pair(grad))
            dk_ref[:keys, :] += dot_tn(jnp.concatenate(scores_all, axis=0), split_pair(query_part))
            d_query = d_query * HD ** (-0.5)
            cos_part, sin_part = cos[lower:keys], sin[lower:keys]
            out_ref[lower:keys, cols] = (
                d_query * cos_part - swap_halves(d_query) * sin_part
            ).astype(BF)
    first = iota(dk_ref.shape, 1) < HD
    d_key = dk_ref[...]
    d_key = (d_key + pltpu.roll(d_key, HD, 1)) * HD ** (-0.5)
    d_key = d_key * cos - swap_halves(d_key) * sin
    d_value = dv_ref[...]
    d_value = d_value + pltpu.roll(d_value, HD, 1)
    out_ref[:, width:] = jnp.where(first, d_key, d_value).astype(BF)


def conv_rows(signal, taps_ref, position):
    total = taps_ref[4:5, :] + taps_ref[3:4, :] * signal
    for lag in range(1, 4):
        moved = jnp.where(position >= lag, pltpu.roll(signal, lag, 0), 0.0)
        total = total + taps_ref[3 - lag : 4 - lag, :] * moved
    return total


def conv_back(signal, d_pre, taps_ref, grad_ref, position):
    rows = signal.shape[0]
    grad_ref[...] = jnp.zeros_like(grad_ref)
    grad_ref[4:5, :] = jnp.sum(d_pre, axis=0, keepdims=True)
    grad_ref[3:4, :] = jnp.sum(d_pre * signal, axis=0, keepdims=True)
    total = taps_ref[3:4, :] * d_pre
    for lag in range(1, 4):
        kept = jnp.where(position >= lag, d_pre, 0.0)
        grad_ref[3 - lag : 4 - lag, :] = jnp.sum(
            kept * pltpu.roll(signal, lag, 0), axis=0, keepdims=True
        )
        total = total + taps_ref[3 - lag : 4 - lag, :] * pltpu.roll(kept, rows - lag, 0)
    return total


def softplus(v):
    return jnp.maximum(v, 0.0) + jnp.log1p(jnp.exp(-jnp.abs(v)))


def spread_matrix(width):
    shape = (LANES, width)
    return (iota(shape, 0) == (iota(shape, 1) >> 6)).astype(F32)


def scan_setup(step_ref, heads_ref):
    steps = softplus(step_ref[...] + heads_ref[0:1, :])
    rates = -jnp.exp(heads_ref[1:2, :])
    return steps, rates


def block_decays(steps, rates, segc, lower):
    upper = lower + BLK
    shape = (BLK, BLK)
    lower_ones = (iota(shape, 0) >= iota(shape, 1)).astype(F32)
    decays = dot_nn(lower_ones, steps[lower:upper] * rates, PRECISE)
    seg_part = segc[lower:upper]
    if lower == 0:
        arrive = None
    else:
        carried = seg_part == segc[lower - 1 : lower]
        arrive = jnp.where(carried, jnp.exp(decays), 0.0)
    kept = seg_part == segc[upper - 1 : upper]
    leave = jnp.where(kept, jnp.exp(decays[BLK - 1 : BLK] - decays), 0.0)
    return decays, arrive, leave, lower_ones


def block_mixing(decays, decays_t, head, allowed):
    gap = decays[:, head : head + 1] - decays_t[head : head + 1, :]
    return jnp.exp(jnp.where(allowed, gap, FAR))


def scan_fwd_kernel(
    x_ref, bc_ref, step_ref, tapx_ref, tapbc_ref, heads_ref, skip_ref, segc_ref, segr_ref,
    pos_ref, out_ref, states_ref,
):
    rows, width = x_ref.shape
    position = pos_ref[...]
    segc, segr = segc_ref[...], segr_ref[...]
    conv_x = jax.nn.silu(conv_rows(x_ref[...], tapx_ref, position)).astype(BF)
    conv_bc = jax.nn.silu(conv_rows(bc_ref[...], tapbc_ref, position)).astype(BF)
    steps, rates = scan_setup(step_ref, heads_ref)
    spread = spread_matrix(width)
    scaled = conv_x.astype(F32) * dot_nn(steps, spread, PRECISE)
    state = None
    for lower in range(0, rows, BLK):
        upper = lower + BLK
        b_part = conv_bc[lower:upper, :LANES]
        c_part = conv_bc[lower:upper, LANES:]
        decays, arrive, leave, lower_ones = block_decays(steps, rates, segc, lower)
        decays_t = decays.T
        allowed = (segc[lower:upper] == segr[:, lower:upper]) & (lower_ones > 0.0)
        inner = dot_nt(c_part, b_part)
        scaled_part = scaled[lower:upper]
        scaled_low = scaled_part.astype(BF)
        fresh = dot_tn(b_part, (scaled_part * dot_nn(leave, spread, PRECISE)).astype(BF))
        if state is None:
            recall = None
            states_ref[lower // BLK] = jnp.zeros(fresh.shape, F32)
            state = fresh
        else:
            arrive_wide = dot_nn(arrive, spread, PRECISE)
            recall = dot_nn(c_part, state.astype(BF)) * arrive_wide
            states_ref[lower // BLK] = state
            state = state * arrive_wide[BLK - 1 : BLK] + fresh
        for pair in range(width // LANES):
            cols = slice(pair * LANES, (pair + 1) * LANES)
            mixes = [
                (block_mixing(decays, decays_t, 2 * pair + side, allowed) * inner).astype(BF)
                for side in range(2)
            ]
            local = dot_nn(jnp.concatenate(mixes, axis=1), split_pair(scaled_low[:, cols]))
            if recall is not None:
                local = local + recall[:, cols]
            out_ref[lower:upper, cols] = local + skip_ref[0:1, cols] * conv_x[
                lower:upper, cols
            ].astype(F32)


def scan_bwd_kernel(
    x_ref, bc_ref, step_ref, tapx_ref, tapbc_ref, heads_ref, skip_ref, segc_ref, segr_ref,
    pos_ref, states_ref, dy_ref, out_ref, gtapx_ref, gtapbc_ref, gheads_ref, dx_ref, dbc_ref,
):
    rows, width = x_ref.shape
    position = pos_ref[...]
    segc, segr = segc_ref[...], segr_ref[...]
    pre_x = conv_rows(x_ref[...], tapx_ref, position)
    pre_bc = conv_rows(bc_ref[...], tapbc_ref, position)
    conv_x = jax.nn.silu(pre_x).astype(BF)
    conv_bc = jax.nn.silu(pre_bc).astype(BF)
    steps, rates = scan_setup(step_ref, heads_ref)
    spread = spread_matrix(width)
    steps_wide = dot_nn(steps, spread, PRECISE)
    lane = iota((BLK, LANES), 1)
    sub = iota((LANES, BLK), 0)
    last_row = iota((BLK, LANES), 0) == BLK - 1
    d_state = None
    g_bias = jnp.zeros((1, LANES), F32)
    g_rate = jnp.zeros((1, LANES), F32)
    g_skip = jnp.zeros((1, width), F32)
    for lower in range(rows - BLK, -1, -BLK):
        upper = lower + BLK
        b_part = conv_bc[lower:upper, :LANES]
        c_part = conv_bc[lower:upper, LANES:]
        decays, arrive, leave, lower_ones = block_decays(steps, rates, segc, lower)
        decays_t = decays.T
        allowed = (segc[lower:upper] == segr[:, lower:upper]) & (lower_ones > 0.0)
        inner = dot_nt(c_part, b_part)
        x_part = conv_x[lower:upper].astype(F32)
        scaled_part = x_part * steps_wide[lower:upper]
        scaled_low = scaled_part.astype(BF)
        grad = dy_ref[lower:upper, :]
        grad_low = grad.astype(BF)
        d_scaled = []
        d_inner = jnp.zeros((BLK, BLK), F32)
        row_sums = jnp.zeros((BLK, LANES), F32)
        col_sums = jnp.zeros((LANES, BLK), F32)
        for pair in range(width // LANES):
            cols = slice(pair * LANES, (pair + 1) * LANES)
            grad_pair = split_pair(grad_low[:, cols])
            d_mix = dot_nt(grad_pair, scaled_low[:, cols])
            mixes = []
            for side in range(2):
                head = 2 * pair + side
                mixing = block_mixing(decays, decays_t, head, allowed)
                mix = mixing * inner
                d_part = d_mix[side * BLK : (side + 1) * BLK]
                d_inner = d_inner + d_part * mixing
                both = d_part * mix
                row_sums = jnp.where(lane == head, jnp.sum(both, axis=1, keepdims=True), row_sums)
                col_sums = jnp.where(sub == head, jnp.sum(both, axis=0, keepdims=True), col_sums)
                mixes.append(mix.astype(BF))
            d_scaled.append(dot_tn(jnp.concatenate(mixes, axis=0), grad_pair))
        d_scaled = jnp.concatenate(d_scaled, axis=1)
        d_decays = row_sums - col_sums.T
        d_inner = d_inner.astype(BF)
        d_c = dot_nn(d_inner, b_part)
        d_b = dot_tn(d_inner, c_part)
        if lower > 0:
            arrive_wide = dot_nn(arrive, spread, PRECISE)
            state = states_ref[lower // BLK]
            state_low = state.astype(BF)
            recall = dot_nn(c_part, state_low) * arrive_wide
            d_decays = d_decays + dot_nt(recall * grad, spread, PRECISE)
            grad_in = (grad * arrive_wide).astype(BF)
            d_c = d_c + dot_nt(grad_in, state_low)
        if d_state is not None:
            state_grad = d_state.astype(BF)
            leave_wide = dot_nn(leave, spread, PRECISE)
            d_kept = dot_nn(b_part, state_grad) * leave_wide
            d_b = d_b + dot_nt((scaled_part * leave_wide).astype(BF), state_grad)
            d_leave = dot_nt(d_kept * scaled_part, spread, PRECISE)
            d_last = jnp.sum(d_leave, axis=0, keepdims=True)
            if lower > 0:
                lingering = jnp.sum(d_state * state, axis=0, keepdims=True)
                lingering = lingering * arrive_wide[BLK - 1 : BLK]
                d_last = d_last + dot_nt(
                    jnp.broadcast_to(lingering, (8, width)), spread, PRECISE
                )[0:1]
            d_decays = d_decays - d_leave + jnp.where(last_row, d_last, 0.0)
            d_scaled = d_scaled + d_kept
        if lower > 0:
            d_new = dot_tn(c_part, grad_in)
            if d_state is None:
                d_state = d_new
            else:
                d_state = d_state * arrive_wide[BLK - 1 : BLK] + d_new
        d_log = dot_tn(lower_ones, d_decays, PRECISE)
        steps_part = steps[lower:upper]
        d_steps = dot_nt(d_scaled * x_part, spread, PRECISE) + d_log * rates
        d_step_in = d_steps * jax.nn.sigmoid(step_ref[lower:upper, :] + heads_ref[0:1, :])
        g_bias = g_bias + jnp.sum(d_step_in, axis=0, keepdims=True)
        g_rate = g_rate + jnp.sum(d_log * steps_part, axis=0, keepdims=True) * rates
        g_skip = g_skip + jnp.sum(grad * x_part, axis=0, keepdims=True)
        out_ref[lower:upper, width + 2 * LANES :] = d_step_in.astype(BF)
        dx_ref[lower:upper, :] = d_scaled * steps_wide[lower:upper] + grad * skip_ref[0:1, :]
        dbc_ref[lower:upper, :LANES] = d_b
        dbc_ref[lower:upper, LANES:] = d_c
    gheads_ref[...] = jnp.zeros_like(gheads_ref)
    gheads_ref[0:1, :] = g_bias
    gheads_ref[1:2, :] = g_rate
    gheads_ref[2:3, :] = dot_nt(jnp.broadcast_to(g_skip, (8, width)), spread, PRECISE)[0:1]
    gate = jax.nn.sigmoid(pre_x)
    d_pre = dx_ref[...] * gate * (1.0 + pre_x * (1.0 - gate))
    out_ref[:, :width] = conv_back(x_ref[...], d_pre, tapx_ref, gtapx_ref, position).astype(BF)
    gate = jax.nn.sigmoid(pre_bc)
    d_pre = dbc_ref[...] * gate * (1.0 + pre_bc * (1.0 - gate))
    out_ref[:, width : width + 2 * LANES] = conv_back(
        bc_ref[...], d_pre, tapbc_ref, gtapbc_ref, position
    ).astype(BF)


VMEM_BYTES = 48 * 1024 * 1024


def column_block(rows, width, index):
    return pl.BlockSpec((rows, width), lambda i: (0, index))


def whole_block(shape):
    zeros = (0,) * len(shape)
    return pl.BlockSpec(shape, lambda i: zeros)


def single_step(kernel, in_specs, outs, scratch=(), flops=1000000):
    return pl.pallas_call(
        kernel,
        grid=(1,),
        in_specs=in_specs,
        out_specs=[whole_block(o.shape) for o in outs],
        out_shape=outs,
        scratch_shapes=list(scratch),
        compiler_params=pltpu.CompilerParams(vmem_limit_bytes=VMEM_BYTES),
        cost_estimate=pl.CostEstimate(flops=flops, bytes_accessed=4000000, transcendentals=0),
    )


def attention_specs(rows, width, gate_width):
    return [
        column_block(rows, width, gate_width // width),
        column_block(rows, LANES, (gate_width + width) // LANES),
        whole_block((rows, LANES)),
        whole_block((rows, LANES)),
        whole_block((rows, 1)),
        whole_block((1, rows)),
    ]


def attention_fwd(y_a, width, gate_width, cos, sin, segc, segr):
    rows = y_a.shape[0]
    return single_step(
        attention_fwd_kernel,
        attention_specs(rows, width, gate_width),
        [jax.ShapeDtypeStruct((rows, width), BF)],
        flops=3000000000,
    )(y_a, y_a, cos, sin, segc, segr)[0]


def attention_bwd(y_a, width, gate_width, cos, sin, segc, segr, d_attn):
    rows = y_a.shape[0]
    return single_step(
        attention_bwd_kernel,
        attention_specs(rows, width, gate_width) + [whole_block((rows, width))],
        [jax.ShapeDtypeStruct((rows, width + LANES), BF)],
        [pltpu.VMEM((rows, LANES), F32), pltpu.VMEM((rows, LANES), F32)],
        flops=8000000000,
    )(y_a, y_a, cos, sin, segc, segr, d_attn)[0]


def scan_specs(rows, width):
    return [
        column_block(rows, width, 0),
        column_block(rows, 2 * LANES, width // (2 * LANES)),
        column_block(rows, LANES, (width + 2 * LANES) // LANES),
        whole_block((8, width)),
        whole_block((8, 2 * LANES)),
        whole_block((8, LANES)),
        whole_block((1, width)),
        whole_block((rows, 1)),
        whole_block((1, rows)),
        whole_block((rows, 1)),
    ]


def scan_fwd(y_b, width, taps_x, taps_bc, heads, skip, segc, segr, position):
    rows = y_b.shape[0]
    return single_step(
        scan_fwd_kernel,
        scan_specs(rows, width),
        [
            jax.ShapeDtypeStruct((rows, width), F32),
            jax.ShapeDtypeStruct((rows // BLK, LANES, width), F32),
        ],
        flops=6000000000,
    )(y_b, y_b, y_b, taps_x, taps_bc, heads, skip, segc, segr, position)


def scan_bwd(y_b, width, taps_x, taps_bc, heads, skip, segc, segr, position, states, d_out):
    rows = y_b.shape[0]
    return single_step(
        scan_bwd_kernel,
        scan_specs(rows, width)
        + [whole_block(states.shape), whole_block((rows, width))],
        [
            jax.ShapeDtypeStruct(y_b.shape, BF),
            jax.ShapeDtypeStruct((8, width), F32),
            jax.ShapeDtypeStruct((8, 2 * LANES), F32),
            jax.ShapeDtypeStruct((8, LANES), F32),
        ],
        [pltpu.VMEM((rows, width), F32), pltpu.VMEM((rows, 2 * LANES), F32)],
        flops=15000000000,
    )(y_b, y_b, y_b, taps_x, taps_bc, heads, skip, segc, segr, position, states, d_out)


CORE_SWAP = [(0, 1), (1, 0), (2, 3), (3, 2)]
CHIP_SWAP = [(0, 2), (2, 0), (1, 3), (3, 1)]
PAIR_SWAP = [(0, 1), (1, 0)]
QUARTERS = (0, 2, 1, 3)
MOST_ROTATIONS = 8


def core_swap(v):
    return lax.ppermute(v, "ctx", CORE_SWAP)


def chip_swap(v):
    return lax.ppermute(v, "ctx", CHIP_SWAP)


def pair_swap(v):
    return lax.ppermute(v, "tp", PAIR_SWAP)


def rotate(v, by):
    size = lax.axis_size("fsdp")
    return lax.ppermute(v, "fsdp", [(i, (i + by) % size) for i in range(size)])


def few_shards():
    return lax.axis_size("fsdp") <= MOST_ROTATIONS


def quarter_perm(width):
    size = lax.axis_size("fsdp")
    shard = width // size
    piece = shard // 4
    spots = jnp.arange(width, dtype=jnp.int32)
    slot = spots // (size * piece)
    turn = (spots // piece) % size
    within = spots % piece
    quarter = jnp.where(slot == 1, 2, jnp.where(slot == 2, 1, slot)) ^ lax.axis_index("ctx")
    if few_shards():
        owner = lax.rem(lax.axis_index("fsdp") - turn + size, size)
    else:
        owner = turn
    column = owner * shard + quarter * piece + within
    return (spots[:, None] == column[None, :]).astype(BF)


def gather_rows(shard):
    piece = shard.shape[0] // 4
    own = lax.dynamic_slice_in_dim(shard, lax.axis_index("ctx") * piece, piece, 0)
    if few_shards():
        line = [own] + [rotate(own, by) for by in range(1, lax.axis_size("fsdp"))]
        line = jnp.concatenate(line, axis=0)
    else:
        line = lax.all_gather(own, "fsdp", axis=0, tiled=True)
    half = jnp.concatenate([line, chip_swap(line)], axis=0)
    return jnp.concatenate([half, core_swap(half)], axis=0)


def add_low(left, *others):
    total = left.astype(F32)
    for other in others:
        total = total + other.astype(F32)
    return total.astype(BF)


def reduce_rows(whole):
    half = whole.shape[0] // 2
    whole = add_low(whole[:half], core_swap(whole[half:]))
    half = half // 2
    line = add_low(whole[:half], chip_swap(whole[half:]))
    size = lax.axis_size("fsdp")
    if few_shards():
        piece = half // size
        parts = [line[by * piece : (by + 1) * piece] for by in range(size)]
        return add_low(parts[0], *[rotate(parts[by], size - by) for by in range(1, size)])
    return lax.psum_scatter(line, "fsdp", scatter_dimension=0, tiled=True)


def share_quarters(part):
    pair = (part, chip_swap(part))
    others = (core_swap(pair[0]), core_swap(pair[1]))
    by_gap = (pair[0], others[0], pair[1], others[1])
    index = lax.axis_index("ctx")
    core_bit, chip_bit = (index & 1) == 1, (index & 2) == 2
    rows = []
    for quarter in range(4):
        near = jnp.where(core_bit, by_gap[quarter ^ 1], by_gap[quarter])
        far = jnp.where(core_bit, by_gap[quarter ^ 3], by_gap[quarter ^ 2])
        rows.append(jnp.where(chip_bit, far, near))
    return jnp.concatenate(rows, axis=0).astype(F32)


def reduce_small(v):
    v = v + core_swap(v)
    v = v + chip_swap(v)
    if few_shards():
        total = v
        for by in range(1, lax.axis_size("fsdp")):
            total = total + rotate(v, by)
        return total
    return lax.psum(v, "fsdp")


def gather_small(v):
    size = lax.axis_size("fsdp")
    if not few_shards():
        return lax.all_gather(v, "fsdp", axis=0).astype(F32)
    rows = jnp.stack([v] + [rotate(v, by) for by in range(1, size)], axis=0)
    owner = jnp.arange(size, dtype=jnp.int32)
    turn = lax.rem(lax.axis_index("fsdp") - owner + size, size)
    chosen = (turn[:, None] == owner[None, :]).astype(BF)
    return dot_nn(chosen, rows)


def gather_group(rows):
    near = [rows, pair_swap(rows), chip_swap(rows)]
    near.append(lax.ppermute(rows, ("ctx", "tp"), [(i, i ^ 5) for i in range(8)]))
    near = jnp.concatenate(near, axis=0)
    return jnp.concatenate([near, core_swap(near)], axis=0)


def stack_spot(spot, rows):
    member = spot // rows
    gap = (member // 2) ^ lax.axis_index("ctx")
    turn = (member % 2) ^ lax.axis_index("tp")
    return ((gap & 1) * 4 + (gap >> 1) * 2 + turn) * rows + spot % rows


def pick_rows(spots, stack):
    numbers = jnp.arange(stack.shape[0], dtype=jnp.int32)
    chosen = (spots[:, None] == numbers[None, :]).astype(BF)
    return dot_nn(chosen, stack).astype(BF)


def dealt_order(lengths, dealing):
    numbers = jnp.arange(lengths.shape[0], dtype=jnp.int32)
    given_start = jnp.cumsum(lengths, dtype=jnp.int32) - lengths
    chosen = (dealing[:, None] == numbers[None, :]).astype(jnp.int32)
    dealt_len = jnp.sum(chosen * lengths[None, :], axis=1, dtype=jnp.int32)
    dealt_from = jnp.sum(chosen * given_start[None, :], axis=1, dtype=jnp.int32)
    dealt_start = jnp.cumsum(dealt_len, dtype=jnp.int32) - dealt_len
    return dealt_len, dealt_from, dealt_start


def look_up(spots, starts, counts, *tables):
    inside = (
        (spots[:, None] >= starts[None, :]) & (spots[:, None] < (starts + counts)[None, :])
    ).astype(jnp.int32)
    return [jnp.sum(inside * table[None, :], axis=1, dtype=jnp.int32) for table in tables]


def norm_back(grad_out, unit_rows, inverse, gain):
    scaled = grad_out * gain
    return inverse * (scaled - unit_rows * jnp.mean(scaled * unit_rows, axis=1, keepdims=True))


def inverse_norm(rows):
    return lax.rsqrt(jnp.mean(rows * rows, axis=1, keepdims=True) + EPSILON)


def padded(v, rows, cols):
    return jnp.pad(v, ((0, rows - v.shape[0]), (0, cols - v.shape[1])))


def per_device(
    tokens,
    cotangent,
    lengths,
    dealing,
    norm_in,
    w_query,
    w_keyval,
    w_attn_out,
    w_zx,
    w_bc,
    w_step,
    head_params,
    taps_x,
    taps_bc,
    gain_mamba,
    w_mamba_out,
    norm_mid,
    w_gate_up,
    w_down,
):
    tok_rows, model_width = tokens.shape
    tp_size = lax.axis_size("tp")
    fsdp_size = lax.axis_size("fsdp")
    rank_rows = tok_rows * tp_size
    tp_index = lax.axis_index("tp")
    fsdp_index = lax.axis_index("fsdp")
    ctx_index = lax.axis_index("ctx")
    shard = w_query.shape[0]
    heads = head_params.shape[1]
    scan_width = heads * HD
    query_width = w_query.shape[1]
    bc_width = w_bc.shape[1]
    ffn_width = w_gate_up.shape[2]
    own_start = tp_index * tok_rows
    peer_start = (tp_size - 1) * tok_rows - own_start

    dealt_len, dealt_from, dealt_start = dealt_order(lengths[0], dealing[0])
    numbers = jnp.arange(lengths.shape[1], dtype=jnp.int32)
    spots = ctx_index * rank_rows + jnp.arange(rank_rows, dtype=jnp.int32)
    segment, begins, anchor = look_up(
        spots, dealt_start, dealt_len, numbers, dealt_start, dealt_from
    )
    position = spots - begins
    sources = stack_spot(anchor + position, tok_rows)
    home = (ctx_index * tp_size + tp_index) * tok_rows + jnp.arange(tok_rows, dtype=jnp.int32)
    home_dealt, home_given = look_up(home, dealt_from, dealt_len, dealt_start, dealt_from)
    home_spots = stack_spot(home - home_given + home_dealt, tok_rows)
    segc, segr, posc = segment[:, None], segment[None, :], position[:, None]
    half_width = HD // 2
    freqs = ROPE_BASE ** (-jnp.arange(half_width, dtype=jnp.float32) / half_width)
    angles = position.astype(jnp.float32)[:, None] * freqs[None, :]
    cosine, sine = jnp.cos(angles), jnp.sin(angles)
    cos_table = jnp.concatenate([cosine] * 4, axis=1)
    sin_table = jnp.concatenate([-sine, sine, -sine, sine], axis=1)
    perm = quarter_perm(model_width)

    token_stack = gather_group(tokens)
    small = jnp.concatenate(
        [v.reshape(-1) for v in (norm_in, norm_mid, taps_x, taps_bc, gain_mamba)]
    )
    small_sizes = [v.size for v in (norm_in, norm_mid, taps_x, taps_bc, gain_mamba)]
    w_scan = gather_rows(
        jnp.concatenate([w_zx[:, 1, :], w_bc, padded(w_step, shard, LANES)], axis=1)
    )
    w_gate = gather_rows(
        jnp.concatenate([w_zx[:, 0, :], w_query, w_keyval.reshape(shard, -1)], axis=1)
    )
    w_out = gather_rows(jnp.concatenate([w_attn_out, w_mamba_out], axis=0).T)
    w_ffn = gather_rows(w_gate_up.reshape(shard, -1))
    w_back = gather_rows(w_down.T)
    cot_stack = gather_group(cotangent)

    small = gather_small(small)
    ends = [sum(small_sizes[: i + 1]) for i in range(len(small_sizes))]
    smalls = [small[:, end - size : end] for end, size in zip(ends, small_sizes)]
    gains = jnp.stack([smalls[0].reshape(-1), smalls[1].reshape(-1)], axis=0).astype(BF)
    gains = dot_nn(gains, perm)
    gain_in, gain_mid = gains[0:1], gains[1:2]
    taps_one = smalls[2].reshape((fsdp_size,) + taps_x.shape).transpose(1, 2, 0, 3)
    taps_one = padded(taps_one.reshape(taps_x.shape[0], -1), 8, scan_width)
    taps_two = smalls[3].reshape((fsdp_size,) + taps_bc.shape).transpose(1, 0, 2)
    taps_two = padded(taps_two.reshape(taps_bc.shape[0], -1), 8, bc_width)
    gain_flat = smalls[4].reshape((fsdp_size,) + gain_mamba.shape).transpose(1, 0, 2)
    gain_flat = gain_flat.reshape(1, -1)
    heads_pad = padded(head_params, 8, LANES)
    skip = jnp.repeat(head_params[2], HD)[None, :]

    x_rows = dot_nn(pick_rows(sources, token_stack), perm)
    cot_rows = dot_nn(pick_rows(sources, cot_stack), perm).astype(BF)
    inverse_in = inverse_norm(x_rows)
    unit_in = x_rows * inverse_in
    normed_in = (unit_in * gain_in).astype(BF)
    y_scan = dot_nn(normed_in, w_scan)
    y_gate = dot_nn(normed_in, w_gate)
    scan_args = (taps_one, taps_two, heads_pad, skip, segc, segr, posc)
    scan_out, states = scan_fwd(y_scan, scan_width, *scan_args)
    attn_args = (query_width, scan_width, cos_table, sin_table, segc, segr)
    attn_rows = attention_fwd(y_gate, *attn_args)
    gate_in = y_gate[:, :scan_width]
    sigma_in = jax.nn.sigmoid(gate_in)
    gated = scan_out * gate_in * sigma_in
    square_sum = jnp.sum(gated * gated, axis=1)
    square_sum = (square_sum + pair_swap(square_sum))[:, None]
    channels = scan_width * tp_size
    inverse_gate = lax.rsqrt(square_sum / channels + EPSILON)
    unit_gate = gated * inverse_gate
    mamba_rows = (unit_gate * gain_flat).astype(BF)
    branch_rows = jnp.concatenate([attn_rows, mamba_rows], axis=1)
    mixer = dot_nt(branch_rows, w_out).astype(BF)
    mixer = mixer.astype(F32) + pair_swap(mixer).astype(F32)
    hidden = x_rows + mixer
    inverse_mid = inverse_norm(hidden)
    unit_mid = hidden * inverse_mid
    normed_mid = (unit_mid * gain_mid).astype(BF)
    gate_up = dot_nn(normed_mid, w_ffn)
    gate_val, up_val = gate_up[:, :ffn_width], gate_up[:, ffn_width:]
    sigma = jax.nn.sigmoid(gate_val)
    activated = (gate_val * sigma * up_val).astype(BF)

    d_act = dot_nn(cot_rows, w_back)
    d_gate = d_act * up_val * sigma * (1.0 + gate_val * (1.0 - sigma))
    d_up = d_act * gate_val * sigma
    d_gate_up = jnp.concatenate([d_gate, d_up], axis=1).astype(BF)
    d_mid = dot_nt(d_gate_up, w_ffn).astype(BF)
    d_mid = d_mid.astype(F32) + pair_swap(d_mid).astype(F32)
    q_ffn = reduce_rows(dot_tn(normed_mid, d_gate_up).astype(BF))
    q_back = reduce_rows(dot_tn(cot_rows, activated).astype(BF))

    ffn_part = dot_nt(activated, w_back).astype(BF)
    ffn_own = lax.dynamic_slice_in_dim(ffn_part, own_start, tok_rows, 0).astype(F32)
    ffn_peer = pair_swap(lax.dynamic_slice_in_dim(ffn_part, peer_start, tok_rows, 0))
    hidden_own = lax.dynamic_slice_in_dim(hidden, own_start, tok_rows, 0)
    out_own = (hidden_own + ffn_own + ffn_peer.astype(F32)).astype(BF)
    out_stack = gather_group(dot_nt(out_own, perm).astype(BF))
    mixed_home = pick_rows(home_spots, out_stack)

    d_hidden = cot_rows.astype(F32) + norm_back(d_mid, unit_mid, inverse_mid, gain_mid)
    g_norm_mid = jnp.sum(d_mid * unit_mid, axis=0, keepdims=True)
    d_mix = d_hidden.astype(BF)
    d_branch = dot_nn(d_mix, w_out).astype(BF)
    q_out = reduce_rows(dot_tn(d_mix, branch_rows).astype(BF))
    d_attn = d_branch[:, :query_width]
    d_mamba = d_branch[:, query_width:].astype(F32)
    scaled_gate = d_mamba * gain_flat
    gate_stat = jnp.sum(scaled_gate * unit_gate, axis=1)
    gate_stat = (gate_stat + pair_swap(gate_stat))[:, None]
    d_query = attention_bwd(y_gate, *attn_args, d_attn)
    g_gain = jnp.sum(d_mamba * unit_gate, axis=0, keepdims=True)
    d_gated = inverse_gate * (scaled_gate - unit_gate * (gate_stat / channels))
    d_scan = d_gated * gate_in * sigma_in
    d_z = d_gated * scan_out * sigma_in * (1.0 + gate_in * (1.0 - sigma_in))
    dy_gate = jnp.concatenate([d_z.astype(BF), d_query], axis=1)
    q_gate = reduce_rows(dot_tn(normed_in, dy_gate).astype(BF))
    dy_scan, g_taps_one, g_taps_two, g_heads = scan_bwd(
        y_scan, scan_width, *scan_args, states, d_scan
    )
    d_in = (dot_nt(dy_gate, w_gate) + dot_nt(dy_scan, w_scan)).astype(BF)
    q_scan = reduce_rows(dot_tn(normed_in, dy_scan).astype(BF))
    d_in_own = lax.dynamic_slice_in_dim(d_in, own_start, tok_rows, 0).astype(F32)
    d_in_peer = pair_swap(lax.dynamic_slice_in_dim(d_in, peer_start, tok_rows, 0))
    d_in_own = d_in_own + d_in_peer.astype(F32)

    def own_rows(v):
        return lax.dynamic_slice_in_dim(v, own_start, tok_rows, 0)

    unit_own = own_rows(unit_in)
    grad_own = own_rows(d_hidden) + norm_back(d_in_own, unit_own, own_rows(inverse_in), gain_in)
    g_norm_in = jnp.sum(d_in_own * unit_own, axis=0, keepdims=True)
    grad_stack = gather_group(dot_nt(grad_own.astype(BF), perm).astype(BF))
    grad_home = pick_rows(home_spots, grad_stack)

    s_ffn = share_quarters(q_ffn)
    s_back = share_quarters(q_back)
    s_out = share_quarters(q_out)
    s_gate = share_quarters(q_gate)
    q_bc = q_scan[:, scan_width : scan_width + bc_width]
    q_bc = add_low(q_bc, pair_swap(q_bc))
    q_scan = jnp.concatenate(
        [q_scan[:, :scan_width], q_bc, q_scan[:, scan_width + bc_width :]], axis=1
    )
    s_scan = share_quarters(q_scan)
    g_norms = dot_nt(
        jnp.concatenate([g_norm_in, g_norm_mid], axis=0), perm.astype(F32), PRECISE
    )
    g_norms, g_taps_two = g_norms.reshape(-1), g_taps_two[: taps_bc.shape[0]].reshape(-1)
    g_taps_one = g_taps_one[: taps_x.shape[0]].reshape(-1)
    g_heads = g_heads[:3, :heads].reshape(-1)
    g_gain = g_gain.reshape(-1)
    parts = (g_norms[:model_width], g_taps_two, g_norms[model_width:], g_taps_one, g_heads, g_gain)
    paired = model_width + g_taps_two.shape[0]
    sums = reduce_small(jnp.concatenate(parts))
    sums = jnp.concatenate([sums[:paired] + pair_swap(sums[:paired]), sums[paired:]])
    ends = [sum(v.size for v in parts[: i + 1]) for i in range(len(parts))]
    sum_in, sum_two, sum_mid, sum_one, sum_heads, sum_gain = [
        sums[end - v.size : end] for end, v in zip(ends, parts)
    ]

    def shard_of(array, dim_index):
        piece = array.shape[dim_index] // fsdp_size
        return lax.dynamic_slice_in_dim(array, fsdp_index * piece, piece, dim_index)

    return (
        mixed_home,
        grad_home,
        shard_of(sum_in, 0),
        s_gate[:, scan_width : scan_width + query_width],
        s_gate[:, scan_width + query_width :].reshape(w_keyval.shape),
        s_out[:, :query_width].T,
        jnp.stack([s_gate[:, :scan_width], s_scan[:, :scan_width]], axis=1),
        s_scan[:, scan_width : scan_width + bc_width],
        s_scan[:, scan_width + bc_width :][:, : w_step.shape[1]],
        sum_heads.reshape(head_params.shape),
        shard_of(sum_one.reshape(taps_x.shape[0], heads, HD), 2),
        shard_of(sum_two.reshape(taps_bc.shape[0], -1), 1),
        shard_of(sum_gain.reshape(heads, HD), 1),
        s_out[:, query_width:].T,
        shard_of(sum_mid, 0),
        s_ffn.reshape(w_gate_up.shape),
        s_back.T,
    )


def solution(mesh):
    rows = P(("fsdp", "ctx", "tp"), None)
    in_specs = (
        rows,
        rows,
        P("fsdp", None),
        P("fsdp", None),
        P("fsdp"),
        P("fsdp", "tp"),
        P("fsdp", "tp", None),
        P("tp", "fsdp"),
        P("fsdp", None, "tp"),
        P("fsdp", None),
        P("fsdp", "tp"),
        P(None, "tp"),
        P(None, "tp", "fsdp"),
        P(None, "fsdp"),
        P("tp", "fsdp"),
        P("tp", "fsdp"),
        P("fsdp"),
        P("fsdp", None, "tp"),
        P("tp", "fsdp"),
    )
    out_specs = (
        rows,
        rows,
        P("fsdp"),
        P("fsdp", "tp"),
        P("fsdp", "tp", None),
        P("tp", "fsdp"),
        P("fsdp", None, "tp"),
        P("fsdp", None),
        P("fsdp", "tp"),
        P(None, "tp"),
        P(None, "tp", "fsdp"),
        P(None, "fsdp"),
        P("tp", "fsdp"),
        P("tp", "fsdp"),
        P("fsdp"),
        P("fsdp", None, "tp"),
        P("tp", "fsdp"),
    )
    return jax.shard_map(
        per_device, mesh=mesh, in_specs=in_specs, out_specs=out_specs, check_vma=False
    )
```

time: 1260 us -> 667 us (0.53)
  waiting for transfers between devices: 514 us -> 276 us
  blocking collectives: 201 us -> 0 us
  starting transfers between devices: 1.86 us -> 121 us
  local copies, waits for them, and re-layouts: 226 us -> 109 us
  other arithmetic: 137 us -> 46.1 us
  matrix products: 147 us -> 59 us
  Pallas kernels: 0 us -> 41.7 us
  between operations: 16.7 us -> 2.5 us
    ppermute x0 -> x97, waiting for transfers between devices: none -> 276 us  [the longest x20 107 us: chip_swap(): return lax.ppermute(v, 'ctx', CHIP_SWAP)]
    psum x5 -> x0, waiting for transfers between devices: 247 us -> none  [the longest x1 127 us: per_device(): lax.psum((g_norm_in, g_norm_mid, wide_heads, g_bc, g_taps_bc, wide_taps,...]
    reduce_scatter x11 -> x0, waiting for transfers between devices: 227 us -> none  [the longest x1 79 us: per_device(): lax.psum_scatter(large_grads[6].astype(jnp.bfloat16), 'fsdp', scatter_dim...]
    all_gather x10 -> x0, blocking collectives: 144 us -> none  [the longest x1 19.9 us: per_device(): lax.all_gather(w_bc, 'fsdp', axis=0, tiled=True)]
    ppermute x0 -> x97, starting transfers between devices: none -> 121 us  [the longest x36 77.9 us: rotate(): return lax.ppermute(v, 'fsdp', [(i, (i + by) % size) for i in range(size)])]
    dot_general x97 -> x24, matrix products: 147 us -> 59 us  [the longest x11 31.3 us: dot_nn(): lax.dot_general(a, b, (((1,), (0,)), ((), ())), precision=precision, pref...]
    dynamic_update_slice x15 -> x0, local copies, waits for them, and re-layouts: 86.4 us -> none  [the longest x12 85.9 us: state_space(): final_carry, outputs = lax.scan(jax.checkpoint(advance), start, pieces)]
    psum x4 -> x0, blocking collectives: 57 us -> none  [the longest x1 41.1 us: per_device(): lax.psum((g_norm_in, g_norm_mid, wide_heads, g_bc, g_taps_bc, wide_taps,...]
  transfers between devices with their start and end apart: 22 -> 97, of which waited for: 12 -> 38; matrix products, arithmetic and copies ran while one was open for 36% -> 28% of each run, Pallas kernels for 0% -> 6%
where the time goes in v1:
time: 667 us; the launch traced here: 656 us
  waiting for transfers between devices  276 us (41%)
  starting transfers between devices  121 us (18%)
  local copies, waits for them, and re-layouts  109 us (16%)
  matrix products  59 us (9%)
  other arithmetic  46.1 us (7%)
  Pallas kernels  41.7 us (6%)
    ppermute x20, waiting for transfers between devices, chip_swap(): return lax.ppermute(v, 'ctx', CHIP_SWAP)  107 us
    ppermute x36, starting transfers between devices, rotate(): return lax.ppermute(v, 'fsdp', [(i, (i + by) % size) for i in range(size)])  77.9 us
    ppermute x12, waiting for transfers between devices, pair_swap(): return lax.ppermute(v, 'tp', PAIR_SWAP)  71.2 us
    ppermute x36, waiting for transfers between devices, rotate(): return lax.ppermute(v, 'fsdp', [(i, (i + by) % size) for i in range(size)])  68.3 us
    unnamed x161, local copies, waits for them, and re-layouts  43 us
    dot_general x11, matrix products, dot_nn(): lax.dot_general(a, b, (((1,), (0,)), ((), ())), precision=precision, pref...  31.3 us
    ppermute x4, waiting for transfers between devices, gather_group(): lax.ppermute(rows, ('ctx', 'tp'), [(i, i ^ 5) for i in range(8)])  28.4 us
    ppermute x20, starting transfers between devices, chip_swap(): return lax.ppermute(v, 'ctx', CHIP_SWAP)  19.1 us
  transfers between devices with their start and end apart: 97, of which 38 were waited for; matrix products, arithmetic and copies ran while one was open for 28% of the time, Pallas kernels for 6%

profile of v1, /device:TPU:0, one launch (start us, length us, event | category | flops | bytes accessed | tf_op | source)
XLA Modules:
  0.0 655.7 jit_solution(8320967281951330558)
XLA Ops:
  41.2 9.0 %collective-permute-start.12 = (bf16[64,1152]{1,0:T(8,128)(2,1)}, bf16[64,1152]{1,0:T(8,128)(2,1)S(1)}, u32[]{:S(2)}, u32[]{:S(2)}) collective-permute-start(bf16[64,1152]{1,0:T(8,128)(2,1)} %copy-done.32), channel_id=1, source_target_pairs={{0,8},{8,16},{16,24},{24,0},{1,9},{9,17},{17,25},{25,1},{2,10},{10... | collective-permute-start | bytes 442376 | tf_op jit(solution)/shard_map/ppermute | solution.py:483
  53.2 16.5 %collective-permute-done.30 = bf16[64,1024]{0,1:T(8,128)(2,1)S(1)} collective-permute-done((bf16[64,1024]{0,1:T(8,128)(2,1)S(1)}, bf16[64,1024]{0,1:T(8,128)(2,1)S(1)}, u32[]{:S(2)}, u32[]{:S(2)}) %collective-permute-start.30) | collective-permute-done | bytes 131104 | tf_op jit(solution)/shard_map/ppermute | solution.py:483
  69.7 6.9 %collective-permute-start.13 = (bf16[64,1152]{1,0:T(8,128)(2,1)}, bf16[64,1152]{1,0:T(8,128)(2,1)S(1)}, u32[]{:S(2)}, u32[]{:S(2)}) collective-permute-start(bf16[64,1152]{1,0:T(8,128)(2,1)} %copy-done.32), channel_id=1, source_target_pairs={{0,16},{8,24},{16,0},{24,8},{1,17},{9,25},{17,1},{25,9},{2,18},{10... | collective-permute-start | bytes 442376 | tf_op jit(solution)/shard_map/ppermute | solution.py:483
  77.0 3.4 collective-permute-start.14
  81.1 10.9 %collective-permute-done.13 = bf16[64,1152]{1,0:T(8,128)(2,1)S(1)} collective-permute-done((bf16[64,1152]{1,0:T(8,128)(2,1)}, bf16[64,1152]{1,0:T(8,128)(2,1)S(1)}, u32[]{:S(2)}, u32[]{:S(2)}) %collective-permute-start.13) | collective-permute-done | bytes 147488 | tf_op jit(solution)/shard_map/ppermute | solution.py:483
  93.6 3.3 collective-permute-start.8
  117.0 6.3 collective-permute-done
  126.2 8.7 %collective-permute-done.2 = bf16[256,1024]{1,0:T(8,128)(2,1)S(1)} collective-permute-done((bf16[256,1024]{1,0:T(8,128)(2,1)S(1)}, bf16[256,1024]{1,0:T(8,128)(2,1)S(1)}, u32[]{:S(2)}, u32[]{:S(2)}) %collective-permute-start.2) | collective-permute-done | bytes 524320 | tf_op jit(solution)/shard_map/ppermute | solution.py:577
  137.2 5.4 collective-permute-done.39
  146.7 9.7 %collective-permute-done.32 = bf16[256,1024]{0,1:T(8,128)(2,1)} collective-permute-done((bf16[256,1024]{0,1:T(8,128)(2,1)S(1)}, bf16[256,1024]{0,1:T(8,128)(2,1)}, u32[]{:S(2)}, u32[]{:S(2)}) %collective-permute-start.32) | collective-permute-done | bytes 524320 | tf_op jit(solution)/shard_map/ppermute | solution.py:474
  159.8 9.3 %collective-permute-done.15 = bf16[256,1152]{1,0:T(8,128)(2,1)} collective-permute-done((bf16[256,1152]{1,0:T(8,128)(2,1)S(1)}, bf16[256,1152]{1,0:T(8,128)(2,1)}, u32[]{:S(2)}, u32[]{:S(2)}) %collective-permute-start.15) | collective-permute-done | bytes 589856 | tf_op jit(solution)/shard_map/ppermute | solution.py:474
  170.0 4.0 concatenate.160
  173.9 4.0 concatenate.166
  180.1 35.3 %collective-permute-done.40 = bf16[256,1024]{1,0:T(8,128)(2,1)} collective-permute-done((bf16[256,1024]{1,0:T(8,128)(2,1)}, bf16[256,1024]{1,0:T(8,128)(2,1)}, u32[]{:S(2)}, u32[]{:S(2)}) %collective-permute-start.40) | collective-permute-done | bytes 524320 | tf_op jit(solution)/shard_map/ppermute | solution.py:474
  215.5 9.8 %collective-permute-done.41 = bf16[256,1024]{1,0:T(8,128)(2,1)} collective-permute-done((bf16[256,1024]{1,0:T(8,128)(2,1)}, bf16[256,1024]{1,0:T(8,128)(2,1)}, u32[]{:S(2)}, u32[]{:S(2)}) %collective-permute-start.41) | collective-permute-done | bytes 524320 | tf_op jit(solution)/shard_map/ppermute | solution.py:577
  240.9 5.0 concatenate.161
  246.0 5.0 concatenate.167
  255.0 4.0 constant_dynamic-update-slice_fusion
  259.0 5.8 multiply_reduce_fusion.3
  271.4 15.0 %shard_map.315 = (f32[512,768]{1,0:T(8,128)S(1)}, f32[4,128,768]{2,1,0:T(8,128)S(1)}) custom-call(f32[512,1152]{1,0:T(8,128)S(1)} %fusion.121.x_ref.bc_ref.step_ref, f32[512,1152]{1,0:T(8,128)S(1)} %fusion.121.x_ref.bc_ref.step_ref, f32[512,1152]{1,0:T(8,128)S(1)} %fusion.121.x_ref.bc_ref.step_ref, f32[8,768]{1,0:T(8,128)S(1)} %pad.17.tapx_ref, ...), custom_call_target="tpu_custom_call" | custom-call | flops 6000000000 | bytes 4000000 | tf_op jit(solution)/shard_map/pallas_call | solution.py:434
  289.0 4.1 shard_map.314
  300.7 6.7 %fusion.26 = bf16[512,1024]{1,0:T(8,128)(2,1)} fusion(s32[1024]{0:T(1024)S(1)} %fusion.74, bf16[2048,1024]{1,0:T(8,128)(2,1)} %copy-done.48, s32[512]{0:T(512)S(1)} %get-tuple-element.198), kind=kOutput, calls=%fused_computation.68 | convolution fusion | flops 3224371200 | bytes 5249024 | tf_op jit(solution)/shard_map/dot_general | solution.py:20
  307.5 3.3 constant_dynamic-update-slice_fusion.32
  310.8 15.0 %collective-permute-done.23 = bf16[512,1024]{1,0:T(8,128)(2,1)} collective-permute-done((bf16[512,1024]{1,0:T(8,128)(2,1)}, bf16[512,1024]{1,0:T(8,128)(2,1)}, u32[]{:S(2)}, u32[]{:S(2)}) %collective-permute-start.23) | collective-permute-done | bytes 1048608 | tf_op jit(solution)/shard_map/ppermute | solution.py:478
  327.9 4.7 fusion.107
  336.9 4.5 convolution_convert_fusion.8
  343.0 8.2 %collective-permute-done.34 = bf16[256,1024]{1,0:T(8,128)(2,1)S(1)} collective-permute-done((bf16[256,1024]{1,0:T(8,128)(2,1)S(1)}, bf16[256,1024]{1,0:T(8,128)(2,1)S(1)}, u32[]{:S(2)}, u32[]{:S(2)}) %collective-permute-start.34) | collective-permute-done | bytes 524320 | tf_op jit(solution)/shard_map/ppermute | solution.py:478
  363.4 31.0 %collective-permute-done.35 = bf16[256,1024]{1,0:T(8,128)(2,1)S(1)} collective-permute-done((bf16[256,1024]{1,0:T(8,128)(2,1)S(1)}, bf16[256,1024]{1,0:T(8,128)(2,1)S(1)}, u32[]{:S(2)}, u32[]{:S(2)}) %collective-permute-start.35) | collective-permute-done | bytes 524320 | tf_op jit(solution)/shard_map/ppermute | solution.py:478
  405.4 5.5 shard_map.316
  416.7 17.2 %shard_map.317 = (bf16[512,1152]{1,0:T(8,128)(2,1)S(1)}, f32[8,768]{1,0:T(8,128)S(1)}, f32[8,256]{1,0:T(8,128)S(1)}, f32[8,128]{1,0:T(8,128)S(1)}) custom-call(f32[512,1152]{1,0:T(8,128)} %copy-done.4, f32[512,1152]{1,0:T(8,128)} %copy-done.4, f32[512,1152]{1,0:T(8,128)} %copy-done.4, f32[8,768]{1,0:T(8,128)S(1)} %pad.17.tapx_ref, ...), custom_call_target="tpu_custom_call" | custom-call | flops 15000000512 | bytes 4000000 | tf_op jit(solution)/shard_map/pallas_call | solution.py:447
  458.0 3.4 collective-permute-done.51
  462.6 3.7 collective-permute-start.53
  466.3 3.6 constant_dynamic-update-slice_fusion.52
  470.5 3.8 collective-permute-start.92
  474.5 3.7 collective-permute-done.93
  478.2 3.2 collective-permute-done.92
  508.1 9.9 %collective-permute-done.48 = bf16[256,1024]{1,0:T(8,128)(2,1)S(1)} collective-permute-done((bf16[256,1024]{1,0:T(8,128)(2,1)S(1)}, bf16[256,1024]{1,0:T(8,128)(2,1)S(1)}, u32[]{:S(2)}, u32[]{:S(2)}) %collective-permute-start.48) | collective-permute-done | bytes 524320 | tf_op jit(solution)/shard_map/ppermute | solution.py:577
  522.6 6.6 %collective-permute-done.65 = bf16[256,1024]{1,0:T(8,128)(2,1)S(1)} collective-permute-done((bf16[256,1024]{1,0:T(8,128)(2,1)S(1)}, bf16[256,1024]{1,0:T(8,128)(2,1)S(1)}, u32[]{:S(2)}, u32[]{:S(2)}) %collective-permute-start.65) | collective-permute-done | bytes 524320 | tf_op jit(solution)/shard_map/ppermute | solution.py:474
  546.6 29.2 %collective-permute-done.57 = bf16[256,1152]{1,0:T(8,128)(2,1)S(1)} collective-permute-done((bf16[256,1152]{1,0:T(8,128)(2,1)S(1)}, bf16[256,1152]{1,0:T(8,128)(2,1)S(1)}, u32[]{:S(2)}, u32[]{:S(2)}) %collective-permute-start.57) | collective-permute-done | bytes 589856 | tf_op jit(solution)/shard_map/ppermute | solution.py:474
  575.8 3.9 collective-permute-start.74
  580.5 3.5 collective-permute-done.74
  584.0 4.3 collective-permute-start.58
  588.6 4.0 collective-permute-done.59
  611.7 3.4 collective-permute-start.84
  618.0 3.7 collective-permute-done.85
  621.7 10.7 %collective-permute-done.84 = bf16[64,2048]{1,0:T(8,128)(2,1)S(1)} collective-permute-done((bf16[64,2048]{1,0:T(8,128)(2,1)S(1)}, bf16[64,2048]{1,0:T(8,128)(2,1)S(1)}, u32[]{:S(2)}, u32[]{:S(2)}) %collective-permute-start.84) | collective-permute-done | bytes 262176 | tf_op jit(solution)/shard_map/ppermute | solution.py:483
  633.3 7.4 %collective-permute-done.86 = bf16[64,2048]{1,0:T(8,128)(2,1)S(1)} collective-permute-done((bf16[64,2048]{1,0:T(8,128)(2,1)S(1)}, bf16[64,2048]{1,0:T(8,128)(2,1)S(1)}, u32[]{:S(2)}, u32[]{:S(2)}) %collective-permute-start.86) | collective-permute-done | bytes 262176 | tf_op jit(solution)/shard_map/ppermute | solution.py:474
  650.9 4.3 fusion.28
  (511 shorter events, 263.4 us)
Async XLA Ops:
  1.9 31.4 %collective-permute-start.18 = (bf16[64,1024]{0,1:T(8,128)(2,1)S(1)}, bf16[64,1024]{0,1:T(8,128)(2,1)S(1)}, u32[]{:S(2)}, u32[]{:S(2)}) collective-permute-start(bf16[64,1024]{0,1:T(8,128)(2,1)S(1)} %fusion.43), channel_id=1, source_target_pairs={{0,8},{8,16},{16,24},{24,0},{1,9},{9,17},{17,25},{25,1},{2,10},{10... | collective-permute-start | bytes 393224 | tf_op jit(solution)/shard_map/ppermute | solution.py:483
  5.0 34.4 %collective-permute-start.19 = (bf16[64,1024]{0,1:T(8,128)(2,1)S(1)}, bf16[64,1024]{0,1:T(8,128)(2,1)S(1)}, u32[]{:S(2)}, u32[]{:S(2)}) collective-permute-start(bf16[64,1024]{0,1:T(8,128)(2,1)S(1)} %fusion.43), channel_id=1, source_target_pairs={{0,16},{8,24},{16,0},{24,8},{1,17},{9,25},{17,1},{25,9},{2,18},{10... | collective-permute-start | bytes 393224 | tf_op jit(solution)/shard_map/ppermute | solution.py:483
  12.7 17.8 %collective-permute-start.5 = (bf16[1984]{0:T(1024)(128)(2,1)S(1)}, bf16[1984]{0:T(1024)(128)(2,1)S(1)}, u32[]{:S(2)}, u32[]{:S(2)}) collective-permute-start(bf16[1984]{0:T(1024)(128)(2,1)S(1)} %concatenate.146), channel_id=1, source_target_pairs={{0,16},{8,24},{16,0},{24,8},{1,17},{9,25},{17,1},{25,9},{2,18},{10... | collective-permute-start | bytes 11912 | tf_op jit(solution)/shard_map/ppermute | solution.py:483
  12.9 17.7 %collective-permute-start.4 = (bf16[1984]{0:T(1024)(128)(2,1)S(1)}, bf16[1984]{0:T(1024)(128)(2,1)S(1)}, u32[]{:S(2)}, u32[]{:S(2)}) collective-permute-start(bf16[1984]{0:T(1024)(128)(2,1)S(1)} %concatenate.146), channel_id=1, source_target_pairs={{0,8},{8,16},{16,24},{24,0},{1,9},{9,17},{17,25},{25,1},{2,10},{10... | collective-permute-start | bytes 11912 | tf_op jit(solution)/shard_map/ppermute | solution.py:483
  30.5 20.2 %collective-permute-start.29 = (bf16[64,1024]{0,1:T(8,128)(2,1)S(1)}, bf16[64,1024]{0,1:T(8,128)(2,1)S(1)}, u32[]{:S(2)}, u32[]{:S(2)}) collective-permute-start(bf16[64,1024]{0,1:T(8,128)(2,1)S(1)} %dynamic-slice_bitcast_fusion), channel_id=1, source_target_pairs={{0,8},{8,16},{16,24},{24,0},{1,9},{9,17},{17,25},{25,1},{2,10},{10... | collective-permute-start | bytes 393224 | tf_op jit(solution)/shard_map/ppermute | solution.py:483
  30.5 39.1 %collective-permute-start.30 = (bf16[64,1024]{0,1:T(8,128)(2,1)S(1)}, bf16[64,1024]{0,1:T(8,128)(2,1)S(1)}, u32[]{:S(2)}, u32[]{:S(2)}) collective-permute-start(bf16[64,1024]{0,1:T(8,128)(2,1)S(1)} %dynamic-slice_bitcast_fusion), channel_id=1, source_target_pairs={{0,16},{8,24},{16,0},{24,8},{1,17},{9,25},{17,1},{25,9},{2,18},{10... | collective-permute-start | bytes 393224 | tf_op jit(solution)/shard_map/ppermute | solution.py:483
  33.2 36.4 %collective-permute-start.31 = (bf16[64,1024]{0,1:T(8,128)(2,1)S(1)}, bf16[64,1024]{0,1:T(8,128)(2,1)S(1)}, u32[]{:S(2)}, u32[]{:S(2)}) collective-permute-start(bf16[64,1024]{0,1:T(8,128)(2,1)S(1)} %dynamic-slice_bitcast_fusion), channel_id=1, source_target_pairs={{0,24},{8,0},{16,8},{24,16},{1,25},{9,1},{17,9},{25,17},{2,26},{10... | collective-permute-start | bytes 393224 | tf_op jit(solution)/shard_map/ppermute | solution.py:483
  39.4 72.2 %collective-permute-start.24 = (bf16[64,2048]{1,0:T(8,128)(2,1)S(1)}, bf16[64,2048]{1,0:T(8,128)(2,1)S(1)}, u32[]{:S(2)}, u32[]{:S(2)}) collective-permute-start(bf16[64,2048]{1,0:T(8,128)(2,1)S(1)} %get-tuple-element.121), channel_id=1, source_target_pairs={{0,8},{8,16},{16,24},{24,0},{1,9},{9,17},{17,25},{25,1},{2,10},{10... | collective-permute-start | bytes 786440 | tf_op jit(solution)/shard_map/ppermute | solution.py:483
  41.2 35.7 %collective-permute-start.12 = (bf16[64,1152]{1,0:T(8,128)(2,1)}, bf16[64,1152]{1,0:T(8,128)(2,1)S(1)}, u32[]{:S(2)}, u32[]{:S(2)}) collective-permute-start(bf16[64,1152]{1,0:T(8,128)(2,1)} %copy-done.32), channel_id=1, source_target_pairs={{0,8},{8,16},{16,24},{24,0},{1,9},{9,17},{17,25},{25,1},{2,10},{10... | collective-permute-start | bytes 442376 | tf_op jit(solution)/shard_map/ppermute | solution.py:483
  50.6 62.5 %collective-permute-start.25 = (bf16[64,2048]{1,0:T(8,128)(2,1)S(1)}, bf16[64,2048]{1,0:T(8,128)(2,1)S(1)}, u32[]{:S(2)}, u32[]{:S(2)}) collective-permute-start(bf16[64,2048]{1,0:T(8,128)(2,1)S(1)} %get-tuple-element.121), channel_id=1, source_target_pairs={{0,16},{8,24},{16,0},{24,8},{1,17},{9,25},{17,1},{25,9},{2,18},{10... | collective-permute-start | bytes 786440 | tf_op jit(solution)/shard_map/ppermute | solution.py:483
  69.7 43.9 %collective-permute-start.26 = (bf16[64,2048]{1,0:T(8,128)(2,1)S(1)}, bf16[64,2048]{1,0:T(8,128)(2,1)S(1)}, u32[]{:S(2)}, u32[]{:S(2)}) collective-permute-start(bf16[64,2048]{1,0:T(8,128)(2,1)S(1)} %get-tuple-element.121), channel_id=1, source_target_pairs={{0,24},{8,0},{16,8},{24,16},{1,25},{9,1},{17,9},{25,17},{2,26},{10... | collective-permute-start | bytes 786440 | tf_op jit(solution)/shard_map/ppermute | solution.py:483
  69.7 22.3 %collective-permute-start.13 = (bf16[64,1152]{1,0:T(8,128)(2,1)}, bf16[64,1152]{1,0:T(8,128)(2,1)S(1)}, u32[]{:S(2)}, u32[]{:S(2)}) collective-permute-start(bf16[64,1152]{1,0:T(8,128)(2,1)} %copy-done.32), channel_id=1, source_target_pairs={{0,16},{8,24},{16,0},{24,8},{1,17},{9,25},{17,1},{25,9},{2,18},{10... | collective-permute-start | bytes 442376 | tf_op jit(solution)/shard_map/ppermute | solution.py:483
  111.6 23.3 %collective-permute-start.2 = (bf16[256,1024]{1,0:T(8,128)(2,1)S(1)}, bf16[256,1024]{1,0:T(8,128)(2,1)S(1)}, u32[]{:S(2)}, u32[]{:S(2)}) collective-permute-start(bf16[256,1024]{1,0:T(8,128)(2,1)S(1)} %copy-done.27), channel_id=1, source_target_pairs={{0,5},{1,4},{2,7},{3,6},{4,1},{5,0},{6,3},{7,2},{8,13},{9,12},{10,... | collective-permute-start | bytes 1572872 | tf_op jit(solution)/shard_map/ppermute | solution.py:577
  113.1 29.5 %collective-permute-start.39 = (bf16[256,1024]{1,0:T(8,128)(2,1)}, bf16[256,1024]{1,0:T(8,128)(2,1)}, u32[]{:S(2)}, u32[]{:S(2)}) collective-permute-start(bf16[256,1024]{1,0:T(8,128)(2,1)} %param.20), channel_id=1, source_target_pairs={{0,1},{1,0},{2,3},{3,2},{4,5},{5,4},{6,7},{7,6},{8,9},{9,8},{10,11... | collective-permute-start | bytes 1572872 | tf_op jit(solution)/shard_map/ppermute | solution.py:478
  113.6 32.0 %collective-permute-start.21 = (bf16[256,1024]{0,1:T(8,128)(2,1)S(1)}, bf16[256,1024]{0,1:T(8,128)(2,1)}, u32[]{:S(2)}, u32[]{:S(2)}) collective-permute-start(bf16[256,1024]{0,1:T(8,128)(2,1)S(1)} %pad_maximum_fusion.17), channel_id=1, source_target_pairs={{0,4},{4,0},{2,6},{6,2},{1,5},{5,1},{3,7},{7,3},{8,12},{12,8},{10,... | collective-permute-start | bytes 1572872 | tf_op jit(solution)/shard_map/ppermute | solution.py:474
  123.3 33.2 %collective-permute-start.32 = (bf16[256,1024]{0,1:T(8,128)(2,1)S(1)}, bf16[256,1024]{0,1:T(8,128)(2,1)}, u32[]{:S(2)}, u32[]{:S(2)}) collective-permute-start(bf16[256,1024]{0,1:T(8,128)(2,1)S(1)} %pad_maximum_fusion.18), channel_id=1, source_target_pairs={{0,4},{4,0},{2,6},{6,2},{1,5},{5,1},{3,7},{7,3},{8,12},{12,8},{10,... | collective-permute-start | bytes 1572872 | tf_op jit(solution)/shard_map/ppermute | solution.py:474
  124.8 44.3 %collective-permute-start.15 = (bf16[256,1152]{1,0:T(8,128)(2,1)S(1)}, bf16[256,1152]{1,0:T(8,128)(2,1)}, u32[]{:S(2)}, u32[]{:S(2)}) collective-permute-start(bf16[256,1152]{1,0:T(8,128)(2,1)S(1)} %pad_maximum_fusion.16), channel_id=1, source_target_pairs={{0,4},{4,0},{2,6},{6,2},{1,5},{5,1},{3,7},{7,3},{8,12},{12,8},{10,... | collective-permute-start | bytes 1769480 | tf_op jit(solution)/shard_map/ppermute | solution.py:474
  134.9 93.1 %collective-permute-start.27 = (bf16[256,2048]{1,0:T(8,128)(2,1)}, bf16[256,2048]{1,0:T(8,128)(2,1)}, u32[]{:S(2)}, u32[]{:S(2)}) collective-permute-start(bf16[256,2048]{1,0:T(8,128)(2,1)} %pad_maximum_fusion.10), channel_id=1, source_target_pairs={{0,4},{4,0},{2,6},{6,2},{1,5},{5,1},{3,7},{7,3},{8,12},{12,8},{10,... | collective-permute-start | bytes 3145736 | tf_op jit(solution)/shard_map/ppermute | solution.py:474
  142.6 82.7 %collective-permute-start.10 = (bf16[256,1152]{1,0:T(8,128)(2,1)}, bf16[256,1152]{1,0:T(8,128)(2,1)}, u32[]{:S(2)}, u32[]{:S(2)}) collective-permute-start(bf16[256,1152]{1,0:T(8,128)(2,1)} %pad_maximum_fusion.15), channel_id=1, source_target_pairs={{0,4},{4,0},{2,6},{6,2},{1,5},{5,1},{3,7},{7,3},{8,12},{12,8},{10,... | collective-permute-start | bytes 1769480 | tf_op jit(solution)/shard_map/ppermute | solution.py:474
  145.6 69.9 %collective-permute-start.40 = (bf16[256,1024]{1,0:T(8,128)(2,1)}, bf16[256,1024]{1,0:T(8,128)(2,1)}, u32[]{:S(2)}, u32[]{:S(2)}) collective-permute-start(bf16[256,1024]{1,0:T(8,128)(2,1)} %param.20), channel_id=1, source_target_pairs={{0,4},{4,0},{2,6},{6,2},{1,5},{5,1},{3,7},{7,3},{8,12},{12,8},{10,... | collective-permute-start | bytes 1572872 | tf_op jit(solution)/shard_map/ppermute | solution.py:474
  156.5 68.8 %collective-permute-start.41 = (bf16[256,1024]{1,0:T(8,128)(2,1)}, bf16[256,1024]{1,0:T(8,128)(2,1)}, u32[]{:S(2)}, u32[]{:S(2)}) collective-permute-start(bf16[256,1024]{1,0:T(8,128)(2,1)} %param.20), channel_id=1, source_target_pairs={{0,5},{1,4},{2,7},{3,6},{4,1},{5,0},{6,3},{7,2},{8,13},{9,12},{10,... | collective-permute-start | bytes 1572872 | tf_op jit(solution)/shard_map/ppermute | solution.py:577
  169.1 85.9 %collective-permute-start.3 = (bf16[1024,1024]{1,0:T(8,128)(2,1)}, bf16[1024,1024]{1,0:T(8,128)(2,1)}, u32[]{:S(2)}, u32[]{:S(2)}) collective-permute-start(bf16[1024,1024]{1,0:T(8,128)(2,1)} %pad_maximum_fusion), channel_id=1, source_target_pairs={{0,2},{2,0},{4,6},{6,4},{1,3},{3,1},{5,7},{7,5},{8,10},{10,8},{12,... | collective-permute-start | bytes 6291464 | tf_op jit(solution)/shard_map/ppermute | solution.py:470
  215.5 25.0 %collective-permute-start.22 = (bf16[512,1024]{0,1:T(8,128)(2,1)}, bf16[512,1024]{0,1:T(8,128)(2,1)}, u32[]{:S(2)}, u32[]{:S(2)}) collective-permute-start(bf16[512,1024]{0,1:T(8,128)(2,1)} %concatenate.160), channel_id=1, source_target_pairs={{0,2},{2,0},{4,6},{6,4},{1,3},{3,1},{5,7},{7,5},{8,10},{10,8},{12,... | collective-permute-start | bytes 3145736 | tf_op jit(solution)/shard_map/ppermute | solution.py:470
  225.3 20.7 %collective-permute-start.33 = (bf16[512,1024]{0,1:T(8,128)(2,1)}, bf16[512,1024]{0,1:T(8,128)(2,1)}, u32[]{:S(2)}, u32[]{:S(2)}) collective-permute-start(bf16[512,1024]{0,1:T(8,128)(2,1)} %concatenate.166), channel_id=1, source_target_pairs={{0,2},{2,0},{4,6},{6,4},{1,3},{3,1},{5,7},{7,5},{8,10},{10,8},{12,... | collective-permute-start | bytes 3145736 | tf_op jit(solution)/shard_map/ppermute | solution.py:470
  225.3 25.7 %collective-permute-start.16 = (bf16[512,1152]{1,0:T(8,128)(2,1)}, bf16[512,1152]{1,0:T(8,128)(2,1)}, u32[]{:S(2)}, u32[]{:S(2)}) collective-permute-start(bf16[512,1152]{1,0:T(8,128)(2,1)} %get-tuple-element.154), channel_id=1, source_target_pairs={{0,2},{2,0},{4,6},{6,4},{1,3},{3,1},{5,7},{7,5},{8,10},{10,8},{12,... | collective-permute-start | bytes 3538952 | tf_op jit(solution)/shard_map/ppermute | solution.py:470
  228.0 25.5 %collective-permute-start.11 = (bf16[512,1152]{1,0:T(8,128)(2,1)}, bf16[512,1152]{1,0:T(8,128)(2,1)}, u32[]{:S(2)}, u32[]{:S(2)}) collective-permute-start(bf16[512,1152]{1,0:T(8,128)(2,1)} %get-tuple-element.152), channel_id=1, source_target_pairs={{0,2},{2,0},{4,6},{6,4},{1,3},{3,1},{5,7},{7,5},{8,10},{10,8},{12,... | collective-permute-start | bytes 3538952 | tf_op jit(solution)/shard_map/ppermute | solution.py:470
  240.4 52.7 %collective-permute-start.42 = (bf16[1024,1024]{1,0:T(8,128)(2,1)}, bf16[1024,1024]{1,0:T(8,128)(2,1)}, u32[]{:S(2)}, u32[]{:S(2)}) collective-permute-start(bf16[1024,1024]{1,0:T(8,128)(2,1)} %pad_maximum_fusion.2), channel_id=1, source_target_pairs={{0,2},{2,0},{4,6},{6,4},{1,3},{3,1},{5,7},{7,5},{8,10},{10,8},{12,... | collective-permute-start | bytes 6291464 | tf_op jit(solution)/shard_map/ppermute | solution.py:470
  245.9 61.5 %collective-permute-start.28 = (bf16[512,2048]{1,0:T(8,128)(2,1)}, bf16[512,2048]{1,0:T(8,128)(2,1)}, u32[]{:S(2)}, u32[]{:S(2)}) collective-permute-start(bf16[512,2048]{1,0:T(8,128)(2,1)} %get-tuple-element.134), channel_id=1, source_target_pairs={{0,2},{2,0},{4,6},{6,4},{1,3},{3,1},{5,7},{7,5},{8,10},{10,8},{12,... | collective-permute-start | bytes 6291464 | tf_op jit(solution)/shard_map/ppermute | solution.py:470
  300.2 25.6 %collective-permute-start.23 = (bf16[512,1024]{1,0:T(8,128)(2,1)}, bf16[512,1024]{1,0:T(8,128)(2,1)}, u32[]{:S(2)}, u32[]{:S(2)}) collective-permute-start(bf16[512,1024]{1,0:T(8,128)(2,1)} %convolution_convert_fusion.7), channel_id=1, source_target_pairs={{0,1},{1,0},{2,3},{3,2},{4,5},{5,4},{6,7},{7,6},{8,9},{9,8},{10,11... | collective-permute-start | bytes 3145736 | tf_op jit(solution)/shard_map/ppermute | solution.py:478
  341.4 55.2 %collective-permute-start.43 = (bf16[512,1024]{1,0:T(8,128)(2,1)S(1)}, bf16[512,1024]{1,0:T(8,128)(2,1)S(1)}, u32[]{:S(2)}, u32[]{:S(2)}) collective-permute-start(bf16[512,1024]{1,0:T(8,128)(2,1)S(1)} %convolution_convert_fusion.8), channel_id=1, source_target_pairs={{0,1},{1,0},{2,3},{3,2},{4,5},{5,4},{6,7},{7,6},{8,9},{9,8},{10,11... | collective-permute-start | bytes 3145736 | tf_op jit(solution)/shard_map/ppermute | solution.py:478
  352.4 42.1 %collective-permute-start.35 = (bf16[256,1024]{1,0:T(8,128)(2,1)S(1)}, bf16[256,1024]{1,0:T(8,128)(2,1)S(1)}, u32[]{:S(2)}, u32[]{:S(2)}) collective-permute-start(bf16[256,1024]{1,0:T(8,128)(2,1)S(1)} %get-tuple-element.206), channel_id=1, source_target_pairs={{0,1},{1,0},{2,3},{3,2},{4,5},{5,4},{6,7},{7,6},{8,9},{9,8},{10,11... | collective-permute-start | bytes 1572872 | tf_op jit(solution)/shard_map/ppermute | solution.py:478
  352.9 41.5 %collective-permute-start.36 = (bf16[256,1024]{1,0:T(8,128)(2,1)S(1)}, bf16[256,1024]{1,0:T(8,128)(2,1)S(1)}, u32[]{:S(2)}, u32[]{:S(2)}) collective-permute-start(bf16[256,1024]{1,0:T(8,128)(2,1)S(1)} %get-tuple-element.206), channel_id=1, source_target_pairs={{0,4},{4,0},{2,6},{6,2},{1,5},{5,1},{3,7},{7,3},{8,12},{12,8},{10,... | collective-permute-start | bytes 1572872 | tf_op jit(solution)/shard_map/ppermute | solution.py:474
  354.4 40.1 %collective-permute-start.37 = (bf16[256,1024]{1,0:T(8,128)(2,1)S(1)}, bf16[256,1024]{1,0:T(8,128)(2,1)S(1)}, u32[]{:S(2)}, u32[]{:S(2)}) collective-permute-start(bf16[256,1024]{1,0:T(8,128)(2,1)S(1)} %get-tuple-element.206), channel_id=1, source_target_pairs={{0,5},{1,4},{2,7},{3,6},{4,1},{5,0},{6,3},{7,2},{8,13},{9,12},{10,... | collective-permute-start | bytes 1572872 | tf_op jit(solution)/shard_map/ppermute | solution.py:577
  361.1 130.8 %collective-permute-start.81 = (bf16[512,2048]{1,0:T(8,128)(2,1)}, bf16[512,2048]{1,0:T(8,128)(2,1)}, u32[]{:S(2)}, u32[]{:S(2)}) collective-permute-start(bf16[512,2048]{1,0:T(8,128)(2,1)} %slice.391), channel_id=1, source_target_pairs={{0,2},{2,0},{4,6},{6,4},{1,3},{3,1},{5,7},{7,5},{8,10},{10,8},{12,... | collective-permute-start | bytes 6291464 | tf_op jit(solution)/shard_map/ppermute | solution.py:470
  396.0 209.2 %collective-permute-start.38 = (bf16[1024,1024]{1,0:T(8,128)(2,1)}, bf16[1024,1024]{1,0:T(8,128)(2,1)}, u32[]{:S(2)}, u32[]{:S(2)}) collective-permute-start(bf16[1024,1024]{1,0:T(8,128)(2,1)} %pad_maximum_fusion.1), channel_id=1, source_target_pairs={{0,2},{2,0},{4,6},{6,4},{1,3},{3,1},{5,7},{7,5},{8,10},{10,8},{12,... | collective-permute-start | bytes 6291464 | tf_op jit(solution)/shard_map/ppermute | solution.py:470
  413.7 34.9 %collective-permute-start.90 = (bf16[256,1024]{1,0:T(8,128)(2,1)S(1)}, bf16[256,1024]{1,0:T(8,128)(2,1)}, u32[]{:S(2)}, u32[]{:S(2)}) collective-permute-start(bf16[256,1024]{1,0:T(8,128)(2,1)S(1)} %slice.401), channel_id=1, source_target_pairs={{0,4},{4,0},{2,6},{6,2},{1,5},{5,1},{3,7},{7,3},{8,12},{12,8},{10,... | collective-permute-start | bytes 1572872 | tf_op jit(solution)/shard_map/ppermute | solution.py:474
  478.2 18.3 %collective-permute-start.64 = (bf16[512,1024]{1,0:T(8,128)(2,1)}, bf16[512,1024]{1,0:T(8,128)(2,1)}, u32[]{:S(2)}, u32[]{:S(2)}) collective-permute-start(bf16[512,1024]{1,0:T(8,128)(2,1)} %slice.366), channel_id=1, source_target_pairs={{0,2},{2,0},{4,6},{6,4},{1,3},{3,1},{5,7},{7,5},{8,10},{10,8},{12,... | collective-permute-start | bytes 3145736 | tf_op jit(solution)/shard_map/ppermute | solution.py:470
  488.5 31.9 %collective-permute-start.72 = (bf16[512,1152]{1,0:T(8,128)(2,1)}, bf16[512,1152]{1,0:T(8,128)(2,1)}, u32[]{:S(2)}, u32[]{:S(2)}) collective-permute-start(bf16[512,1152]{1,0:T(8,128)(2,1)} %slice.374), channel_id=1, source_target_pairs={{0,2},{2,0},{4,6},{6,4},{1,3},{3,1},{5,7},{7,5},{8,10},{10,8},{12,... | collective-permute-start | bytes 3538952 | tf_op jit(solution)/shard_map/ppermute | solution.py:470
  496.6 21.4 %collective-permute-start.48 = (bf16[256,1024]{1,0:T(8,128)(2,1)S(1)}, bf16[256,1024]{1,0:T(8,128)(2,1)S(1)}, u32[]{:S(2)}, u32[]{:S(2)}) collective-permute-start(bf16[256,1024]{1,0:T(8,128)(2,1)S(1)} %get-tuple-element.208), channel_id=1, source_target_pairs={{0,5},{1,4},{2,7},{3,6},{4,1},{5,0},{6,3},{7,2},{8,13},{9,12},{10,... | collective-permute-start | bytes 1572872 | tf_op jit(solution)/shard_map/ppermute | solution.py:577
  502.9 31.1 %collective-permute-start.56 = (bf16[512,1152]{1,0:T(8,128)(2,1)S(1)}, bf16[512,1152]{1,0:T(8,128)(2,1)S(1)}, u32[]{:S(2)}, u32[]{:S(2)}) collective-permute-start(bf16[512,1152]{1,0:T(8,128)(2,1)S(1)} %copy-done.34), channel_id=1, source_target_pairs={{0,2},{2,0},{4,6},{6,4},{1,3},{3,1},{5,7},{7,5},{8,10},{10,8},{12,... | collective-permute-start | bytes 3538952 | tf_op jit(solution)/shard_map/ppermute | solution.py:470
  506.7 22.5 %collective-permute-start.65 = (bf16[256,1024]{1,0:T(8,128)(2,1)S(1)}, bf16[256,1024]{1,0:T(8,128)(2,1)S(1)}, u32[]{:S(2)}, u32[]{:S(2)}) collective-permute-start(bf16[256,1024]{1,0:T(8,128)(2,1)S(1)} %slice.368), channel_id=1, source_target_pairs={{0,4},{4,0},{2,6},{6,2},{1,5},{5,1},{3,7},{7,3},{8,12},{12,8},{10,... | collective-permute-start | bytes 1572872 | tf_op jit(solution)/shard_map/ppermute | solution.py:474
  522.0 19.8 %collective-permute-start.73 = (bf16[256,1152]{1,0:T(8,128)(2,1)S(1)}, bf16[256,1152]{1,0:T(8,128)(2,1)S(1)}, u32[]{:S(2)}, u32[]{:S(2)}) collective-permute-start(bf16[256,1152]{1,0:T(8,128)(2,1)S(1)} %slice.376), channel_id=1, source_target_pairs={{0,4},{4,0},{2,6},{6,2},{1,5},{5,1},{3,7},{7,3},{8,12},{12,8},{10,... | collective-permute-start | bytes 1769480 | tf_op jit(solution)/shard_map/ppermute | solution.py:474
  537.7 64.1 %collective-permute-start.82 = (bf16[256,2048]{1,0:T(8,128)(2,1)}, bf16[256,2048]{1,0:T(8,128)(2,1)}, u32[]{:S(2)}, u32[]{:S(2)}) collective-permute-start(bf16[256,2048]{1,0:T(8,128)(2,1)} %slice.393), channel_id=1, source_target_pairs={{0,4},{4,0},{2,6},{6,2},{1,5},{5,1},{3,7},{7,3},{8,12},{12,8},{10,... | collective-permute-start | bytes 3145736 | tf_op jit(solution)/shard_map/ppermute | solution.py:474
  541.3 34.5 %collective-permute-start.57 = (bf16[256,1152]{1,0:T(8,128)(2,1)S(1)}, bf16[256,1152]{1,0:T(8,128)(2,1)S(1)}, u32[]{:S(2)}, u32[]{:S(2)}) collective-permute-start(bf16[256,1152]{1,0:T(8,128)(2,1)S(1)} %slice.360), channel_id=1, source_target_pairs={{0,4},{4,0},{2,6},{6,2},{1,5},{5,1},{3,7},{7,3},{8,12},{12,8},{10,... | collective-permute-start | bytes 1769480 | tf_op jit(solution)/shard_map/ppermute | solution.py:474
  542.1 37.8 %collective-permute-start.76 = (bf16[64,1152]{1,0:T(8,128)(2,1)S(1)}, bf16[64,1152]{1,0:T(8,128)(2,1)S(1)}, u32[]{:S(2)}, u32[]{:S(2)}) collective-permute-start(bf16[64,1152]{1,0:T(8,128)(2,1)S(1)} %get-tuple-element.143), channel_id=1, source_target_pairs={{0,8},{8,16},{16,24},{24,0},{1,9},{9,17},{17,25},{25,1},{2,10},{10... | collective-permute-start | bytes 442376 | tf_op jit(solution)/shard_map/ppermute | solution.py:483
  544.3 35.6 %collective-permute-start.75 = (bf16[64,1152]{1,0:T(8,128)(2,1)S(1)}, bf16[64,1152]{1,0:T(8,128)(2,1)S(1)}, u32[]{:S(2)}, u32[]{:S(2)}) collective-permute-start(bf16[64,1152]{1,0:T(8,128)(2,1)S(1)} %get-tuple-element.144), channel_id=1, source_target_pairs={{0,16},{8,24},{16,0},{24,8},{1,17},{9,25},{17,1},{25,9},{2,18},{10... | collective-permute-start | bytes 442376 | tf_op jit(solution)/shard_map/ppermute | solution.py:483
  588.6 59.2 %collective-permute-start.49 = (bf16[1024,1024]{1,0:T(8,128)(2,1)}, bf16[1024,1024]{1,0:T(8,128)(2,1)}, u32[]{:S(2)}, u32[]{:S(2)}) collective-permute-start(bf16[1024,1024]{1,0:T(8,128)(2,1)} %pad_maximum_fusion.4), channel_id=1, source_target_pairs={{0,2},{2,0},{4,6},{6,4},{1,3},{3,1},{5,7},{7,5},{8,10},{10,8},{12,... | collective-permute-start | bytes 6291464 | tf_op jit(solution)/shard_map/ppermute | solution.py:470
  611.7 20.7 %collective-permute-start.84 = (bf16[64,2048]{1,0:T(8,128)(2,1)S(1)}, bf16[64,2048]{1,0:T(8,128)(2,1)S(1)}, u32[]{:S(2)}, u32[]{:S(2)}) collective-permute-start(bf16[64,2048]{1,0:T(8,128)(2,1)S(1)} %get-tuple-element.133), channel_id=1, source_target_pairs={{0,16},{8,24},{16,0},{24,8},{1,17},{9,25},{17,1},{25,9},{2,18},{10... | collective-permute-start | bytes 786440 | tf_op jit(solution)/shard_map/ppermute | solution.py:483
  (111 other events, 953.1 us)
